TPU v7x, 32 devices: a whole 2x2x4 slice. The times are simulated.
32 devices in a mesh: groups: 2 (over y), seq: 4 (over z), head: 4 (over x, core).
Axes of the slice: x: 2, y: 2, z: 4, core: 2. Of those that a mesh axis runs over, the one named last changes fastest.
Arguments:
- layer_queries: bfloat16 [4096, 4096], P(('groups', 'seq'), 'head'), parts along dimension 0, may hold values from -1.75 to 1.75
- layer_keys: bfloat16 [4096, 4096], P(('groups', 'seq'), 'head'), parts along dimension 0, may hold values from -1.75 to 1.75
- layer_values: bfloat16 [4096, 4096], P(('groups', 'seq'), 'head'), parts along dimension 0, may hold values from -6 to 6
- gate_logits: bfloat16 [4096, 4096], P(('groups', 'seq'), 'head'), parts along dimension 0, may hold values from -6 to 6
- norm_gain: bfloat16 [4096], P('head'), may hold values from 0.099609375 to 1.8984375
- decay_exponents: int32 [32], P('head'), may hold values from 0 to 9
- doc_lengths: int32 [8], P('groups'), parts along dimension 0, may hold values from 1 to 1024, 2048 in all
- out_weight: bfloat16 [6144, 4096], P('seq', 'head'), may hold values from -0.125 to 0.125
Outputs:
- layer_output: bfloat16 [4096, 6144], P(('groups', 'seq'), 'head'), parts along dimension 0
There are 2 independent parts, one for each index of `groups`. A program takes and returns all parts, laid end to end along the dimension named above; an argument that names none is the same for every part. Nothing has to cross between parts.
Inputs may be any that keep to these rules, and one draw needn't show every extreme that they name: `doc_lengths`: the lengths sum to 2048.
All inputs are finite; a program needn't handle non-finite values.
Results may differ from a plain program's by a relative error of at most 0.0063.
Values may be sent and summed in bfloat16 or wider, within the bound.
A program may use at most 128 MiB of HBM per device.

v0:
```python
import jax
import jax.numpy as jnp
from jax import lax
from jax.sharding import PartitionSpec as P

HEAD_DIM = 128


def prefix(value, axis, join, neutral):
    count, mine = (lax.axis_size(axis), lax.axis_index(axis))
    pieces = jax.tree.map(lambda part: lax.all_gather(part, axis), value)
    running = jax.tree.map(
        lambda part, zero: jnp.full_like(part, 0) + jnp.asarray(zero, part.dtype), value, neutral
    )

    def turn(position, running):
        longer = join(running, jax.tree.map(lambda part: part[position], pieces))
        return jax.tree.map(lambda new, old: jnp.where(position < mine, new, old), longer, running)

    return lax.fori_loop(0, count - 1, turn, running)


def doc_positions(doc_lengths, first_row, count):
    position = first_row + jnp.arange(count, dtype=jnp.int32)
    starts = jnp.cumsum(doc_lengths) - doc_lengths
    doc_begin = jnp.max(jnp.where(starts[None, :] <= position[:, None], starts[None, :], 0), axis=1)
    return position - doc_begin


def combine(earlier, latter):
    return (earlier[0] * latter[0], latter[0][:, None, None] * earlier[1] + latter[1])


def shards(
    layer_queries,
    layer_keys,
    layer_values,
    gate_logits,
    norm_gain,
    decay_exponents,
    doc_lengths,
    out_weight,
):
    tok_rows = layer_queries.shape[0]
    heads_here = decay_exponents.shape[0]
    token_span = tok_rows * lax.axis_size("seq")
    first_row = lax.axis_index("seq") * tok_rows
    decay_rate = jnp.minimum(jnp.exp2(decay_exponents.astype(jnp.float32)) / token_span, 1.0 / 32.0)
    within = doc_positions(doc_lengths, first_row, tok_rows)
    local_pos = jnp.arange(tok_rows, dtype=jnp.int32)
    query_heads = layer_queries.reshape(tok_rows, heads_here, HEAD_DIM)
    key_heads = layer_keys.reshape(tok_rows, heads_here, HEAD_DIM)
    value_heads = layer_values.reshape(tok_rows, heads_here, HEAD_DIM)
    last_within = within[tok_rows - 1]
    carry_on = jnp.where(last_within >= tok_rows, jnp.exp(-decay_rate * tok_rows), 0.0)
    key_weight = jnp.where(
        (local_pos >= tok_rows - 1 - last_within)[:, None],
        jnp.exp(-decay_rate[None, :] * (tok_rows - local_pos)[:, None].astype(jnp.float32)),
        0.0,
    )
    scaled = (key_heads.astype(jnp.float32) * key_weight[:, :, None]).astype(jnp.bfloat16)
    block_state = jnp.einsum(
        "thd,the->hde", scaled, value_heads, preferred_element_type=jnp.float32
    )
    identity = (jnp.ones_like(carry_on), jnp.zeros_like(block_state))
    incoming_decay, incoming = prefix((carry_on, block_state), "seq", combine, identity)
    lag_grid = local_pos[:, None] - local_pos[None, :]
    valid_mask = (lag_grid >= 0) & (lag_grid <= within[:, None])
    decay_grid = jnp.where(
        valid_mask[None],
        jnp.exp(-decay_rate[:, None, None] * lag_grid[None].astype(jnp.float32)),
        0.0,
    )
    scores = jnp.einsum("thd,shd->hts", query_heads, key_heads, preferred_element_type=jnp.float32)
    weights = (scores * decay_grid).astype(jnp.bfloat16)
    intra_attn = jnp.einsum(
        "hts,shd->thd", weights, value_heads, preferred_element_type=jnp.float32
    )
    incoming_rounded = incoming.astype(jnp.bfloat16)
    query_weight = jnp.where(
        (within >= local_pos + 1)[:, None],
        jnp.exp(-decay_rate[None, :] * local_pos[:, None].astype(jnp.float32)),
        0.0,
    )
    cross_attn = (
        jnp.einsum(
            "thd,hde->the", query_heads, incoming_rounded, preferred_element_type=jnp.float32
        )
        * query_weight[:, :, None]
    )
    attention = (intra_attn + cross_attn).reshape(tok_rows, heads_here * HEAD_DIM)
    squares = lax.psum(jnp.sum(attention * attention, axis=1), "head")
    width_all = heads_here * HEAD_DIM * lax.axis_size("head")
    inv_scale = lax.rsqrt(squares / width_all + 1e-06)
    gated_out = (
        attention
        * inv_scale[:, None]
        * norm_gain.astype(jnp.float32)
        * jax.nn.sigmoid(gate_logits.astype(jnp.float32))
    ).astype(jnp.bfloat16)
    partials = lax.dot_general(
        gated_out,
        lax.all_gather(out_weight, "seq", axis=0, tiled=True),
        (((1,), (1,)), ((), ())),
        preferred_element_type=jnp.float32,
    )
    return lax.psum_scatter(partials, "head", scatter_dimension=1, tiled=True).astype(jnp.bfloat16)


def solution(mesh):
    in_specs = (
        P(("groups", "seq"), "head"),
        P(("groups", "seq"), "head"),
        P(("groups", "seq"), "head"),
        P(("groups", "seq"), "head"),
        P("head"),
        P("head"),
        P("groups"),
        P("seq", "head"),
    )
    out_specs = P(("groups", "seq"), "head")
    return jax.shard_map(shards, mesh=mesh, in_specs=in_specs, out_specs=out_specs, check_vma=False)
```

profile of v0, /device:TPU:11, one launch (start us, length us, event | category | flops | bytes accessed | tf_op | source)
XLA Modules:
  0.0 402.2 jit_solution(6156701245072614927)
XLA Ops:
  6.5 0.0 copy-start
  6.6 0.9 reduce-window.9
  7.5 0.7 bitcast_subtract_fusion
  8.1 0.1 select_reduce_fusion
  8.2 0.6 slice.3
  10.1 1.5 copy.30
  11.7 0.6 dynamic-slice
  12.9 0.1 fusion.31
  13.0 0.1 exponential_select_fusion.1
  13.1 2.5 fusion.9
  15.6 0.0 all-gather.7.cloned.1.call-update
  15.6 0.0 all-gather.5.cloned.1.call-start
  15.7 0.7 all-gather.5.cloned.1.call-update
  16.4 0.0 reduce-scatter.2.cloned.1.call-start
  16.4 7.3 %all-reduce = f32[32]{0:T(128)S(1)} all-reduce(f32[32]{0:T(128)S(1)} %get-tuple-element.132), channel_id=2, replica_groups=mesh['groups'=2,'seq'=4,'head'=4] {'seq'}, use_global_device_ids=true, to_apply=%add | all-reduce | flops 32 | bytes 256
  23.7 0.1 reshape.208
  23.8 1.1 fusion.20
  24.9 0.2 fusion.23
  25.2 6.2 %fusion.1 = f32[8,512,128]{1,2,0:T(8,128)} fusion(f32[512,512]{1,0:T(8,128)} %fusion.20, f32[8]{0:T(128)S(1)} %get-tuple-element.133, pred[512,512]{1,0:T(8,128)(4,1)S(1)} %fusion.23, bf16[512,8,128]{0,2,1:T(8,128)(2,1)S(1)} %bitcast.58, bf16[512,1024]{1,0:T(8,128)(2,1)} %param.12, bf16[512,1024]{1,0:T(8,128)(2,1)S(1)} %copy-done), kind=kOutput, calls=%fused_computation.4 | convolution fusion | flops 1082130432 | bytes 6553632 | tf_op jit(solution)/shard_map/hts,shd->thd/dot_general | solution.py:76
  31.4 29.5 %all-gather.7.cloned.1.call-done = f32[32,128,128]{2,1,0:T(8,128)} async-done(((f32[8,128,128]{2,1,0:T(8,128)}), f32[32,128,128]{2,1,0:T(8,128)}) %all-gather.7.cloned.1.call-update) | async-done | bytes 2097168 | tf_op jit(solution)/shard_map/all_gather | solution.py:11
  60.9 3.6 while.14
  60.9 1.2 fusion.42
  62.2 1.2 fusion.42
  63.4 1.2 fusion.42
  64.6 3.5 multiply_reduce_fusion
  68.1 1.9 copy.28
  70.0 6.1 %psum.7 = f32[512]{0:T(512)S(1)} all-reduce(f32[512]{0:T(512)S(1)} %get-tuple-element.134), channel_id=1, replica_groups=mesh['groups'=2,'seq'=4,'head'=4] {'head'}, use_global_device_ids=true, to_apply=%region_5.6 | all-reduce | flops 512 | bytes 4096 | tf_op jit(solution)/shard_map/psum | solution.py:92
  76.1 202.6 %all-gather.5.cloned.1.call-done = bf16[6144,1024]{1,0:T(8,128)(2,1)} async-done(((bf16[1536,1024]{1,0:T(8,128)(2,1)}), bf16[6144,1024]{1,0:T(8,128)(2,1)}) %all-gather.5.cloned.1.call-update) | async-done | bytes 12582928 | tf_op jit(solution)/shard_map/all_gather | solution.py:103
  278.6 14.6 %fusion.10 = f32[512,6144]{1,0:T(8,128)} fusion(bf16[6144,1024]{1,0:T(8,128)(2,1)} %all-gather.5.cloned.1.call-done, bf16[512,1024]{1,0:T(8,128)(2,1)} %param.13, f32[512,1024]{1,0:T(8,128)S(1)} %copy.28, f32[1024]{0:T(1024)S(1)} %convert_element_type.59, f32[512]{0:T(512)S(1)} %add_rsqrt_fusion), kind=kOutput, calls=%fused_computation.16 | convolution fusion | flops 6446645248 | bytes 28317696 | tf_op jit(solution)/shard_map/dot_general | solution.py:101
  293.2 0.0 reduce-scatter.2.cloned.1.call-update
  293.2 99.2 %reduce-scatter.2.cloned.1.call-done = f32[512,1536]{1,0:T(8,128)} async-done(((f32[512,6144]{1,0:T(8,128)}), f32[512,1536]{1,0:T(8,128)}) %reduce-scatter.2.cloned.1.call-update) | async-done | bytes 3145744 | tf_op jit(solution)/shard_map/reduce_scatter | solution.py:107
  392.5 3.2 convert_element_type.62
  (19 shorter events, 0.1 us)
Async XLA Ops:
  6.5 18.6 %copy-start = (bf16[512,1024]{1,0:T(8,128)(2,1)S(1)}, bf16[512,1024]{1,0:T(8,128)(2,1)}, u32[]{:S(2)}) copy-start(bf16[512,1024]{1,0:T(8,128)(2,1)} %param.10) | copy-start | bytes 3145732
  6.5 5.1 %copy-start.3 = (u32[32]{0:T(128)S(1)}, u32[32]{0:T(128)}, u32[]{:S(2)}) copy-start(u32[32]{0:T(128)} %constant.66) | copy-start | bytes 388
  6.5 6.4 %copy-start.2 = (s32[8]{0:T(128)S(1)}, s32[8]{0:T(128)}, u32[]{:S(2)}) copy-start(s32[8]{0:T(128)} %param.15) | copy-start | bytes 100
  6.5 54.4 %all-gather.7.cloned.1.call-start = ((), (), s32[]{:S(2)}) async-start(), calls=%async_computation.3 | async-start | bytes 2621440 | tf_op jit(solution)/shard_map/all_gather | solution.py:11
  15.6 8.2 %copy-start.1 = (bf16[1024]{0:T(1024)(128)(2,1)S(1)}, bf16[1024]{0:T(1024)(128)(2,1)}, u32[]{:S(2)}) copy-start(bf16[1024]{0:T(1024)(128)(2,1)} %param.14) | copy-start | bytes 6148
  15.6 263.0 %all-gather.5.cloned.1.call-start = ((), (), s32[]{:S(2)}) async-start(), calls=%async_computation.1 | async-start | bytes 15728640 | tf_op jit(solution)/shard_map/all_gather | solution.py:103
  16.4 376.1 %reduce-scatter.2.cloned.1.call-start = ((), (), s32[]{:S(2)}) async-start(), calls=%async_computation.2 | async-start | bytes 15728640 | tf_op jit(solution)/shard_map/reduce_scatter | solution.py:107
Sparse Core Ops, SparseCore 0:
  15.7 45.1 all-gather.6
  62.5 216.0 all-gather.4
  293.3 99.0 reduce-scatter.1
where the time goes:
time: 405 us; the launch traced here: 402 us
  waiting for transfers between devices  332 us (82%)
  matrix products  26.8 us (7%)
  between operations  15.2 us (4%)
  blocking collectives  13.3 us (3%)
  other arithmetic  9.97 us (2%)
  local copies, waits for them, and re-layouts  4.71 us (1%)
    all_gather x1, waiting for transfers between devices, shards(): lax.all_gather(out_weight, 'seq', axis=0, tiled=True)  203 us
    reduce_scatter x1, waiting for transfers between devices, shards(): lax.psum_scatter(partials, 'head', scatter_dimension=1, tiled=True)  99.2 us
    all_gather x1, waiting for transfers between devices, prefix(): pieces = jax.tree.map(lambda part: lax.all_gather(part, axis), value)  29.5 us
    dot_general x1, matrix products, shards(): lax.dot_general(gated_out, lax.all_gather(out_weight, 'seq', axis=0, tile...  14.6 us
  transfers between devices with their start and end apart: 3, of which 3 were waited for; matrix products, arithmetic and copies ran while one was open for 4% of the time, Pallas kernels for 0%

commit v1 on v0

--- a/solution.py
+++ b/solution.py
@@ -22,7 +22,8 @@
 
 def doc_positions(doc_lengths, first_row, count):
     position = first_row + jnp.arange(count, dtype=jnp.int32)
-    starts = jnp.cumsum(doc_lengths) - doc_lengths
+    order = jnp.arange(doc_lengths.shape[0], dtype=jnp.int32)
+    starts = jnp.sum(jnp.where(order[None, :] < order[:, None], doc_lengths[None, :], 0), axis=1)
     doc_begin = jnp.max(jnp.where(starts[None, :] <= position[:, None], starts[None, :], 0), axis=1)
     return position - doc_begin
 

time: 405 us -> 404 us (level)
  no operation moved by 1% of the time
where the time goes in v1:
time: 404 us; the launch traced here: 401 us
  waiting for transfers between devices  332 us (82%)
  matrix products  26.8 us (7%)
  between operations  15.2 us (4%)
  blocking collectives  13.3 us (3%)
  other arithmetic  9.26 us (2%)
  local copies, waits for them, and re-layouts  4.71 us (1%)
    all_gather x1, waiting for transfers between devices, shards(): lax.all_gather(out_weight, 'seq', axis=0, tiled=True)  203 us
    reduce_scatter x1, waiting for transfers between devices, shards(): lax.psum_scatter(partials, 'head', scatter_dimension=1, tiled=True)  99.2 us
    all_gather x1, waiting for transfers between devices, prefix(): pieces = jax.tree.map(lambda part: lax.all_gather(part, axis), value)  29.5 us
    dot_general x1, matrix products, shards(): lax.dot_general(gated_out, lax.all_gather(out_weight, 'seq', axis=0, tile...  14.6 us
  transfers between devices with their start and end apart: 3, of which 3 were waited for; matrix products, arithmetic and copies ran while one was open for 4% of the time, Pallas kernels for 0%

profile of v1, /device:TPU:11, one launch (start us, length us, event | category | flops | bytes accessed | tf_op | source)
XLA Modules:
  0.0 401.5 jit_solution(6566329213834997990)
XLA Ops:
  6.6 0.9 select_reduce_fusion.1
  7.4 0.1 select_reduce_fusion
  7.5 0.6 slice.3
  9.4 1.5 copy.30
  10.9 0.0 copy-done.3
  10.9 0.6 dynamic-slice
  12.2 0.0 copy-done.2
  12.2 0.1 fusion.31
  12.3 0.1 exponential_select_fusion.1
  12.4 2.5 fusion.9
  14.9 0.0 all-gather.7.cloned.1.call-update
  14.9 0.0 all-gather.5.cloned.1.call-start
  15.0 0.7 all-gather.5.cloned.1.call-update
  15.7 0.0 reduce-scatter.2.cloned.1.call-start
  15.7 7.3 %all-reduce = f32[32]{0:T(128)S(1)} all-reduce(f32[32]{0:T(128)S(1)} %get-tuple-element.132), channel_id=2, replica_groups=mesh['groups'=2,'seq'=4,'head'=4] {'seq'}, use_global_device_ids=true, to_apply=%add | all-reduce | flops 32 | bytes 256
  23.0 0.1 reshape.181
  23.1 1.1 fusion.20
  24.2 0.2 fusion.23
  24.5 6.2 %fusion.1 = f32[8,512,128]{1,2,0:T(8,128)} fusion(f32[512,512]{1,0:T(8,128)} %fusion.20, f32[8]{0:T(128)S(1)} %get-tuple-element.133, pred[512,512]{1,0:T(8,128)(4,1)S(1)} %fusion.23, bf16[512,8,128]{0,2,1:T(8,128)(2,1)S(1)} %bitcast.55, bf16[512,1024]{1,0:T(8,128)(2,1)} %param.12, bf16[512,1024]{1,0:T(8,128)(2,1)S(1)} %copy-done), kind=kOutput, calls=%fused_computation.4 | convolution fusion | flops 1082130432 | bytes 6553632 | tf_op jit(solution)/shard_map/hts,shd->thd/dot_general | solution.py:77
  30.7 29.5 %all-gather.7.cloned.1.call-done = f32[32,128,128]{2,1,0:T(8,128)} async-done(((f32[8,128,128]{2,1,0:T(8,128)}), f32[32,128,128]{2,1,0:T(8,128)}) %all-gather.7.cloned.1.call-update) | async-done | bytes 2097168 | tf_op jit(solution)/shard_map/all_gather | solution.py:11
  60.2 3.6 while.14
  60.2 1.2 fusion.42
  61.4 1.2 fusion.42
  62.7 1.2 fusion.42
  63.8 3.5 multiply_reduce_fusion
  67.3 1.9 copy.28
  69.3 6.1 %psum.7 = f32[512]{0:T(512)S(1)} all-reduce(f32[512]{0:T(512)S(1)} %get-tuple-element.134), channel_id=1, replica_groups=mesh['groups'=2,'seq'=4,'head'=4] {'head'}, use_global_device_ids=true, to_apply=%region_5.6 | all-reduce | flops 512 | bytes 4096 | tf_op jit(solution)/shard_map/psum | solution.py:93
  75.3 202.6 %all-gather.5.cloned.1.call-done = bf16[6144,1024]{1,0:T(8,128)(2,1)} async-done(((bf16[1536,1024]{1,0:T(8,128)(2,1)}), bf16[6144,1024]{1,0:T(8,128)(2,1)}) %all-gather.5.cloned.1.call-update) | async-done | bytes 12582928 | tf_op jit(solution)/shard_map/all_gather | solution.py:104
  277.9 14.6 %fusion.10 = f32[512,6144]{1,0:T(8,128)} fusion(bf16[6144,1024]{1,0:T(8,128)(2,1)} %all-gather.5.cloned.1.call-done, bf16[512,1024]{1,0:T(8,128)(2,1)} %param.13, f32[512,1024]{1,0:T(8,128)S(1)} %copy.28, f32[1024]{0:T(1024)S(1)} %convert_element_type.59, f32[512]{0:T(512)S(1)} %add_rsqrt_fusion), kind=kOutput, calls=%fused_computation.16 | convolution fusion | flops 6446645248 | bytes 28317696 | tf_op jit(solution)/shard_map/dot_general | solution.py:102
  292.5 0.0 reduce-scatter.2.cloned.1.call-update
  292.5 99.2 %reduce-scatter.2.cloned.1.call-done = f32[512,1536]{1,0:T(8,128)} async-done(((f32[512,6144]{1,0:T(8,128)}), f32[512,1536]{1,0:T(8,128)}) %reduce-scatter.2.cloned.1.call-update) | async-done | bytes 3145744 | tf_op jit(solution)/shard_map/reduce_scatter | solution.py:108
  391.7 3.2 convert_element_type.62
  (18 shorter events, 0.1 us)
Async XLA Ops:
  6.5 17.9 %copy-start = (bf16[512,1024]{1,0:T(8,128)(2,1)S(1)}, bf16[512,1024]{1,0:T(8,128)(2,1)}, u32[]{:S(2)}) copy-start(bf16[512,1024]{1,0:T(8,128)(2,1)} %param.10) | copy-start | bytes 3145732
  6.5 4.4 %copy-start.3 = (u32[32]{0:T(128)S(1)}, u32[32]{0:T(128)}, u32[]{:S(2)}) copy-start(u32[32]{0:T(128)} %constant.63) | copy-start | bytes 388
  6.5 5.7 %copy-start.2 = (s32[8]{0:T(128)S(1)}, s32[8]{0:T(128)}, u32[]{:S(2)}) copy-start(s32[8]{0:T(128)} %param.15) | copy-start | bytes 100
  6.5 53.7 %all-gather.7.cloned.1.call-start = ((), (), s32[]{:S(2)}) async-start(), calls=%async_computation.3 | async-start | bytes 2621440 | tf_op jit(solution)/shard_map/all_gather | solution.py:11
  14.9 8.2 %copy-start.1 = (bf16[1024]{0:T(1024)(128)(2,1)S(1)}, bf16[1024]{0:T(1024)(128)(2,1)}, u32[]{:S(2)}) copy-start(bf16[1024]{0:T(1024)(128)(2,1)} %param.14) | copy-start | bytes 6148
  14.9 263.0 %all-gather.5.cloned.1.call-start = ((), (), s32[]{:S(2)}) async-start(), calls=%async_computation.1 | async-start | bytes 15728640 | tf_op jit(solution)/shard_map/all_gather | solution.py:104
  15.7 376.1 %reduce-scatter.2.cloned.1.call-start = ((), (), s32[]{:S(2)}) async-start(), calls=%async_computation.2 | async-start | bytes 15728640 | tf_op jit(solution)/shard_map/reduce_scatter | solution.py:108
Sparse Core Ops, SparseCore 0:
  15.0 45.1 all-gather.6
  61.8 216.0 all-gather.4
  292.6 99.0 reduce-scatter.1

commit v2 on v1

v2 whole, which is shorter than its diff:
```python
import jax
import jax.numpy as jnp
from jax import lax
from jax.sharding import PartitionSpec as P

HEAD_DIM = 128
CHUNKS = 2


def doc_positions(doc_lengths, position):
    order = jnp.arange(doc_lengths.shape[0], dtype=jnp.int32)
    starts = jnp.sum(jnp.where(order[None, :] < order[:, None], doc_lengths[None, :], 0), axis=1)
    doc_begin = jnp.max(jnp.where(starts[None, :] <= position[:, None], starts[None, :], 0), axis=1)
    return position - doc_begin


def shards(
    layer_queries,
    layer_keys,
    layer_values,
    gate_logits,
    norm_gain,
    decay_exponents,
    doc_lengths,
    out_weight,
):
    f32 = jnp.float32
    tok_rows = layer_queries.shape[0]
    heads_here = decay_exponents.shape[0]
    seq_count, head_count = lax.axis_size("seq"), lax.axis_size("head")
    mine = lax.axis_index("seq")
    token_span = tok_rows * seq_count
    decay_rate = jnp.minimum(jnp.exp2(decay_exponents.astype(f32)) / token_span, 1.0 / 32.0)
    local_pos = jnp.arange(tok_rows, dtype=jnp.int32)
    within = doc_positions(doc_lengths, mine * tok_rows + local_pos)
    last_within = within[tok_rows - 1]
    query_heads = layer_queries.reshape(tok_rows, heads_here, HEAD_DIM)
    key_heads = layer_keys.reshape(tok_rows, heads_here, HEAD_DIM)
    value_heads = layer_values.reshape(tok_rows, heads_here, HEAD_DIM)

    key_weight = jnp.where(
        (local_pos >= tok_rows - 1 - last_within)[:, None],
        jnp.exp(-decay_rate[None, :] * (tok_rows - local_pos)[:, None].astype(f32)),
        0.0,
    )
    scaled = (key_heads.astype(f32) * key_weight[:, :, None]).astype(jnp.bfloat16)
    block_state = jnp.einsum("thd,the->hde", scaled, value_heads, preferred_element_type=f32)
    states = lax.all_gather(block_state.astype(jnp.bfloat16), "seq")

    blocks = jnp.arange(seq_count, dtype=jnp.int32)
    ends = doc_positions(doc_lengths, blocks * tok_rows + tok_rows - 1)
    carry = jnp.where(
        (ends >= tok_rows)[:, None], jnp.exp(-decay_rate * tok_rows)[None, :], 0.0
    )
    between = (blocks[None, :] > blocks[:, None]) & (blocks[None, :] < mine)
    reach = jnp.prod(jnp.where(between[:, :, None], carry[None], 1.0), axis=1)
    reach = jnp.where((blocks < mine)[:, None], reach, 0.0)

    lag_grid = local_pos[:, None] - local_pos[None, :]
    valid_mask = (lag_grid >= 0) & (lag_grid <= within[:, None])
    decay_grid = jnp.where(
        valid_mask[None], jnp.exp(-decay_rate[:, None, None] * lag_grid[None].astype(f32)), 0.0
    )
    scores = jnp.einsum("thd,shd->hts", query_heads, key_heads, preferred_element_type=f32)
    weights = (scores * decay_grid).astype(jnp.bfloat16)
    intra_attn = jnp.einsum("hts,shd->thd", weights, value_heads, preferred_element_type=f32)
    incoming = jnp.sum(reach[:, :, None, None] * states.astype(f32), axis=0)
    query_weight = jnp.where(
        (within >= local_pos + 1)[:, None],
        jnp.exp(-decay_rate[None, :] * local_pos[:, None].astype(f32)),
        0.0,
    )
    cross_attn = (
        jnp.einsum(
            "thd,hde->the",
            query_heads,
            incoming.astype(jnp.bfloat16),
            preferred_element_type=f32,
        )
        * query_weight[:, :, None]
    )
    attention = (intra_attn + cross_attn).reshape(tok_rows, heads_here * HEAD_DIM)
    squares = lax.psum(jnp.sum(attention * attention, axis=1), "head")
    inv_scale = lax.rsqrt(squares / (heads_here * HEAD_DIM * head_count) + 1e-06)
    gated = attention * norm_gain.astype(f32) * jax.nn.sigmoid(gate_logits.astype(f32))
    contract = (((1,), (1,)), ((), ()))

    if seq_count != head_count:
        partials = lax.dot_general(
            (gated * inv_scale[:, None]).astype(jnp.bfloat16),
            lax.all_gather(out_weight, "seq", axis=0, tiled=True),
            contract,
            preferred_element_type=f32,
        )
        summed = lax.psum_scatter(partials, "head", scatter_dimension=1, tiled=True)
        return summed.astype(jnp.bfloat16)

    gated = gated.astype(jnp.bfloat16)
    swap = [
        (s * head_count + h, h * head_count + s)
        for s in range(seq_count)
        for h in range(head_count)
    ]
    rows = tok_rows // CHUNKS
    pieces = []
    for c in range(CHUNKS):
        everyone = lax.all_gather(gated[c * rows : (c + 1) * rows], "seq", axis=0, tiled=True)
        partials = lax.dot_general(everyone, out_weight, contract, preferred_element_type=f32)
        summed = lax.psum_scatter(
            partials.astype(jnp.bfloat16), "head", scatter_dimension=0, tiled=True
        )
        pieces.append(lax.ppermute(summed, ("seq", "head"), swap))
    out = jnp.concatenate(pieces, axis=0).astype(f32) * inv_scale[:, None]
    return out.astype(jnp.bfloat16)


def solution(mesh):
    split = P(("groups", "seq"), "head")
    in_specs = (split, split, split, split, P("head"), P("head"), P("groups"), P("seq", "head"))
    return jax.shard_map(shards, mesh=mesh, in_specs=in_specs, out_specs=split, check_vma=False)
```

time: 404 us -> 286 us (0.71)
  waiting for transfers between devices: 332 us -> 209 us
  starting transfers between devices: 0.08 us -> 10.8 us
  blocking collectives: 13.3 us -> 5.56 us
    all_gather x2 -> x3, waiting for transfers between devices: 232 us -> 103 us  [the longest x2 83 us: shards(): lax.all_gather(gated[c * rows:(c + 1) * rows], 'seq', axis=0, tiled=True)]
    ppermute x0 -> x2, waiting for transfers between devices: none -> 28.1 us  [shards(): pieces.append(lax.ppermute(summed, ('seq', 'head'), swap))]
    reduce_scatter x1 -> x2, waiting for transfers between devices: 99.2 us -> 77.4 us  [shards(): lax.psum_scatter(partials.astype(jnp.bfloat16), 'head', scatter_dimension...]
    ppermute x0 -> x2, starting transfers between devices: none -> 10.7 us  [shards(): pieces.append(lax.ppermute(summed, ('seq', 'head'), swap))]
    unnamed x1 -> x0, blocking collectives: 7.26 us -> none
    dot_general x4 -> x5, matrix products: 26.8 us -> 26.3 us  [the longest x2 12.9 us: shards(): lax.dot_general(everyone, out_weight, contract, preferred_element_type=f32)]
  transfers between devices with their start and end apart: 3 -> 7, of which waited for: 3 -> 6; matrix products, arithmetic and copies ran while one was open for 4% -> 8% of each run, Pallas kernels for 0% -> 0%
where the time goes in v2:
time: 286 us; the launch traced here: 283 us
  waiting for transfers between devices  209 us (73%)
  matrix products  26.3 us (9%)
  between operations  13.9 us (5%)
  starting transfers between devices  10.8 us (4%)
  other arithmetic  10.5 us (4%)
  local copies, waits for them, and re-layouts  6.81 us (2%)
  blocking collectives  5.56 us (2%)
    all_gather x2, waiting for transfers between devices, shards(): lax.all_gather(gated[c * rows:(c + 1) * rows], 'seq', axis=0, tiled=True)  83 us
    reduce_scatter x2, waiting for transfers between devices, shards(): lax.psum_scatter(partials.astype(jnp.bfloat16), 'head', scatter_dimension...  77.4 us
    ppermute x2, waiting for transfers between devices, shards(): pieces.append(lax.ppermute(summed, ('seq', 'head'), swap))  28.1 us
    all_gather x1, waiting for transfers between devices, shards(): states = lax.all_gather(block_state.astype(jnp.bfloat16), 'seq')  20.2 us
    dot_general x2, matrix products, shards(): lax.dot_general(everyone, out_weight, contract, preferred_element_type=f32)  12.9 us
    ppermute x2, starting transfers between devices, shards(): pieces.append(lax.ppermute(summed, ('seq', 'head'), swap))  10.7 us
    dot_general x1, matrix products, shards(): jnp.einsum('hts,shd->thd', weights, value_heads, preferred_element_type=f32)  6.81 us
  transfers between devices with their start and end apart: 7, of which 6 were waited for; matrix products, arithmetic and copies ran while one was open for 8% of the time, Pallas kernels for 0%

profile of v2, /device:TPU:11, one launch (start us, length us, event | category | flops | bytes accessed | tf_op | source)
XLA Modules:
  0.0 283.3 jit_solution(2266635779119090669)
XLA Ops:
  6.5 0.9 select_reduce_fusion.3
  7.5 0.1 select_reduce_fusion.1
  7.6 0.6 slice.9
  8.8 0.7 multiply_exponential_fusion
  9.5 2.3 copy.29
  11.8 0.1 exponential_select_fusion.1
  11.9 2.7 convolution_convert_fusion.2
  14.7 0.2 select_reduce_fusion.2
  14.9 0.1 broadcast_select_fusion.1
  15.0 0.1 select_reduce_fusion
  15.1 1.1 fusion.15
  16.2 0.1 broadcast_select_fusion
  16.2 0.2 fusion.18
  16.5 6.8 %fusion = f32[8,512,128]{1,2,0:T(8,128)} fusion(f32[512,512]{1,0:T(8,128)} %fusion.15, f32[8]{0:T(128)S(1)} %get-tuple-element.6, pred[512,512]{1,0:T(8,128)(4,1)S(1)} %fusion.18, bf16[512,8,128]{0,2,1:T(8,128)(2,1)} %bitcast.48, bf16[512,1024]{1,0:T(8,128)(2,1)} %param.10, bf16[512,1024]{1,0:T(8,128)(2,1)} %param.8), kind=kOutput, calls=%fused_computation.1 | convolution fusion | flops 1082130432 | bytes 6553632 | tf_op jit(solution)/shard_map/hts,shd->thd/dot_general | solution.py:66
  23.3 20.2 %all-gather.9.cloned.1.call-done = bf16[32,128,128]{2,1,0:T(8,128)(2,1)} async-done(((bf16[8,128,128]{2,1,0:T(8,128)(2,1)}), bf16[32,128,128]{2,1,0:T(8,128)(2,1)}) %all-gather.9.cloned.1.call-update) | async-done | bytes 1048592 | tf_op jit(solution)/shard_map/all_gather | solution.py:48
  43.6 1.5 fusion.7
  45.1 3.9 %multiply_reduce_fusion = (f32[512]{0:T(512)S(1)}, f32[512,8,128]{0,2,1:T(8,128)}) fusion(f32[512,8]{0,1:T(8,128)S(1)} %get-tuple-element.12, bf16[8,128,128]{2,1,0:T(8,128)(2,1)S(1)} %fusion.7, f32[8,512,128]{1,2,0:T(8,128)} %fusion, bf16[512,1024]{1,0:T(8,128)(2,1)} %param.8), kind=kOutput, calls=%fused_computation.14 | convolution fusion | flops 136314368 | bytes 5523456 | tf_op jit(solution)/shard_map/thd,hde->the/dot_general | solution.py:74
  49.0 2.9 %copy.27 = f32[512,1024]{1,0:T(8,128)} copy(f32[512,1024]{0,1:T(8,128)} %bitcast.45) | data formatting | bytes 4194304 | tf_op jit(solution)/shard_map/reshape | solution.py:82
  51.8 2.5 multiply_convert_fusion.3
  54.3 1.0 fusion.29
  55.5 0.7 all-gather.7.cloned.1.call-update
  56.2 43.2 %all-gather.5.cloned.1.call-done = bf16[1024,1024]{1,0:T(8,128)(2,1)} async-done(((bf16[256,1024]{1,0:T(8,128)(2,1)}), bf16[1024,1024]{1,0:T(8,128)(2,1)}) %all-gather.5.cloned.1.call-update) | async-done | bytes 2097168 | tf_op jit(solution)/shard_map/all_gather | solution.py:107
  99.4 6.5 %convolution_convert_fusion.1 = bf16[1024,1536]{1,0:T(8,128)(2,1)} fusion(bf16[1024,1024]{1,0:T(8,128)(2,1)} %all-gather.5.cloned.1.call-done, bf16[1536,1024]{1,0:T(8,128)(2,1)S(1)} %copy-done), kind=kOutput, calls=%fused_computation.7 | convolution fusion | flops 3222798336 | bytes 8388608 | tf_op jit(solution)/shard_map/dot_general | solution.py:108
  106.0 39.7 %all-gather.7.cloned.1.call-done = bf16[1024,1024]{1,0:T(8,128)(2,1)} async-done(((bf16[256,1024]{1,0:T(8,128)(2,1)}), bf16[1024,1024]{1,0:T(8,128)(2,1)}) %all-gather.7.cloned.1.call-update) | async-done | bytes 2097168 | tf_op jit(solution)/shard_map/all_gather | solution.py:107
  145.7 6.5 %convolution_convert_fusion = bf16[1024,1536]{1,0:T(8,128)(2,1)} fusion(bf16[1024,1024]{1,0:T(8,128)(2,1)} %all-gather.7.cloned.1.call-done, bf16[1536,1024]{1,0:T(8,128)(2,1)S(1)} %copy-done), kind=kOutput, calls=%fused_computation.6 | convolution fusion | flops 3222798336 | bytes 8388608 | tf_op jit(solution)/shard_map/dot_general | solution.py:108
  152.2 33.5 %reduce-scatter.3.cloned.1.call-done = bf16[256,1536]{1,0:T(8,128)(2,1)} async-done(((bf16[1024,1536]{1,0:T(8,128)(2,1)}), bf16[256,1536]{1,0:T(8,128)(2,1)}) %reduce-scatter.3.cloned.1.call-update) | async-done | bytes 786448 | tf_op jit(solution)/shard_map/reduce_scatter | solution.py:109
  185.7 4.9 %collective-permute-start = (bf16[256,1536]{1,0:T(8,128)(2,1)}, bf16[256,1536]{1,0:T(8,128)(2,1)}, u32[]{:S(2)}, u32[]{:S(2)}) collective-permute-start(bf16[256,1536]{1,0:T(8,128)(2,1)} %reduce-scatter.3.cloned.1.call-done), channel_id=1, source_target_pairs={{0,0},{1,4},{2,8},{3,12},{4,1},{5,5},{6,9},{7,13},{8,2},{9,6},{10,... | collective-permute-start | bytes 2359304 | tf_op jit(solution)/shard_map/ppermute | solution.py:112
  190.7 43.9 %reduce-scatter.5.cloned.1.call-done = bf16[256,1536]{1,0:T(8,128)(2,1)} async-done(((bf16[1024,1536]{1,0:T(8,128)(2,1)}), bf16[256,1536]{1,0:T(8,128)(2,1)}) %reduce-scatter.5.cloned.1.call-update) | async-done | bytes 786448 | tf_op jit(solution)/shard_map/reduce_scatter | solution.py:109
  234.5 5.7 %collective-permute-start.1 = (bf16[256,1536]{1,0:T(8,128)(2,1)}, bf16[256,1536]{1,0:T(8,128)(2,1)}, u32[]{:S(2)}, u32[]{:S(2)}) collective-permute-start(bf16[256,1536]{1,0:T(8,128)(2,1)} %reduce-scatter.5.cloned.1.call-done), channel_id=1, source_target_pairs={{0,0},{1,4},{2,8},{3,12},{4,1},{5,5},{6,9},{7,13},{8,2},{9,6},{10,... | collective-permute-start | bytes 2359304 | tf_op jit(solution)/shard_map/ppermute | solution.py:112
  240.3 5.6 %psum.7 = f32[512]{0:T(512)S(1)} all-reduce(f32[512]{0:T(512)S(1)} %get-tuple-element.13), channel_id=1, replica_groups=mesh['groups'=2,'seq'=4,'head'=4] {'head'}, use_global_device_ids=true, to_apply=%region_8.9 | all-reduce | flops 512 | bytes 4096 | tf_op jit(solution)/shard_map/psum | solution.py:83
  245.9 28.1 %collective-permute-done.1 = bf16[256,1536]{1,0:T(8,128)(2,1)} collective-permute-done((bf16[256,1536]{1,0:T(8,128)(2,1)}, bf16[256,1536]{1,0:T(8,128)(2,1)}, u32[]{:S(2)}, u32[]{:S(2)}) %collective-permute-start.1) | collective-permute-done | bytes 786464 | tf_op jit(solution)/shard_map/ppermute | solution.py:112
  273.9 2.8 %multiply_convert_fusion.2 = bf16[512,1536]{1,0:T(8,128)(2,1)} fusion(bf16[256,1536]{1,0:T(8,128)(2,1)} %collective-permute-done.1, bf16[256,1536]{1,0:T(8,128)(2,1)} %collective-permute-done, f32[512]{0:T(512)S(1)} %add_rsqrt_fusion), kind=kLoop, calls=%fused_computation.9 | loop fusion | flops 4718592 | bytes 3147776 | tf_op jit(solution)/shard_map/convert_element_type | solution.py:114
  (24 shorter events, 0.3 us)
Async XLA Ops:
  6.5 92.9 %copy-start = (bf16[1536,1024]{1,0:T(8,128)(2,1)S(1)}, bf16[1536,1024]{1,0:T(8,128)(2,1)}, u32[]{:S(2)}) copy-start(bf16[1536,1024]{1,0:T(8,128)(2,1)} %param.15) | copy-start | bytes 9437188
  6.5 37.0 %all-gather.9.cloned.1.call-start = ((), (), s32[]{:S(2)}) async-start(), calls=%async_computation.6 | async-start | bytes 1310720 | tf_op jit(solution)/shard_map/all_gather | solution.py:48
  11.8 3.1 %copy-start.1 = (bf16[1024]{0:T(1024)(128)(2,1)S(1)}, bf16[1024]{0:T(1024)(128)(2,1)}, u32[]{:S(2)}) copy-start(bf16[1024]{0:T(1024)(128)(2,1)} %param.12) | copy-start | bytes 6148
  14.6 84.8 %all-gather.5.cloned.1.call-start = ((), (), s32[]{:S(2)}) async-start(), calls=%async_computation.2 | async-start | bytes 2621440 | tf_op jit(solution)/shard_map/all_gather | solution.py:107
  55.4 90.3 %all-gather.7.cloned.1.call-start = ((), (), s32[]{:S(2)}) async-start(), calls=%async_computation.4 | async-start | bytes 2621440 | tf_op jit(solution)/shard_map/all_gather | solution.py:107
  56.2 129.5 %reduce-scatter.3.cloned.1.call-start = ((), (), s32[]{:S(2)}) async-start(), calls=%async_computation.3 | async-start | bytes 3932160 | tf_op jit(solution)/shard_map/reduce_scatter | solution.py:109
  105.9 128.6 %reduce-scatter.5.cloned.1.call-start = ((), (), s32[]{:S(2)}) async-start(), calls=%async_computation.5 | async-start | bytes 3932160 | tf_op jit(solution)/shard_map/reduce_scatter | solution.py:109
  185.7 60.2 %collective-permute-start = (bf16[256,1536]{1,0:T(8,128)(2,1)}, bf16[256,1536]{1,0:T(8,128)(2,1)}, u32[]{:S(2)}, u32[]{:S(2)}) collective-permute-start(bf16[256,1536]{1,0:T(8,128)(2,1)} %reduce-scatter.3.cloned.1.call-done), channel_id=1, source_target_pairs={{0,0},{1,4},{2,8},{3,12},{4,1},{5,5},{6,9},{7,13},{8,2},{9,6},{10,... | collective-permute-start | bytes 2359304 | tf_op jit(solution)/shard_map/ppermute | solution.py:112
  234.5 39.4 %collective-permute-start.1 = (bf16[256,1536]{1,0:T(8,128)(2,1)}, bf16[256,1536]{1,0:T(8,128)(2,1)}, u32[]{:S(2)}, u32[]{:S(2)}) collective-permute-start(bf16[256,1536]{1,0:T(8,128)(2,1)} %reduce-scatter.5.cloned.1.call-done), channel_id=1, source_target_pairs={{0,0},{1,4},{2,8},{3,12},{4,1},{5,5},{6,9},{7,13},{8,2},{9,6},{10,... | collective-permute-start | bytes 2359304 | tf_op jit(solution)/shard_map/ppermute | solution.py:112
Sparse Core Ops, SparseCore 0:
  14.7 28.8 all-gather.8
  55.5 43.8 all-gather.4
  101.0 44.6 all-gather.6
  148.1 37.5 reduce-scatter.2
  188.2 46.2 reduce-scatter.4

commit v3 on v2

--- a/solution.py
+++ b/solution.py
@@ -45,7 +45,15 @@
     )
     scaled = (key_heads.astype(f32) * key_weight[:, :, None]).astype(jnp.bfloat16)
     block_state = jnp.einsum("thd,the->hde", scaled, value_heads, preferred_element_type=f32)
-    states = lax.all_gather(block_state.astype(jnp.bfloat16), "seq")
+    direct = seq_count == head_count and head_count & (head_count - 1) == 0 and head_count > 1
+    sent_state = block_state.astype(jnp.bfloat16)
+    if direct:
+        states = [
+            lax.ppermute(sent_state, "seq", [(s, s + k) for s in range(seq_count - k)])
+            for k in range(1, seq_count)
+        ]
+    else:
+        states = lax.all_gather(sent_state, "seq")
 
     blocks = jnp.arange(seq_count, dtype=jnp.int32)
     ends = doc_positions(doc_lengths, blocks * tok_rows + tok_rows - 1)
@@ -64,7 +72,13 @@
     scores = jnp.einsum("thd,shd->hts", query_heads, key_heads, preferred_element_type=f32)
     weights = (scores * decay_grid).astype(jnp.bfloat16)
     intra_attn = jnp.einsum("hts,shd->thd", weights, value_heads, preferred_element_type=f32)
-    incoming = jnp.sum(reach[:, :, None, None] * states.astype(f32), axis=0)
+    if direct:
+        incoming = jnp.zeros_like(block_state)
+        for k in range(1, seq_count):
+            far = jnp.where(mine >= k, reach[jnp.maximum(mine - k, 0)], 0.0)
+            incoming += far[:, None, None] * states[k - 1].astype(f32)
+    else:
+        incoming = jnp.sum(reach[:, :, None, None] * states.astype(f32), axis=0)
     query_weight = jnp.where(
         (within >= local_pos + 1)[:, None],
         jnp.exp(-decay_rate[None, :] * local_pos[:, None].astype(f32)),
@@ -80,12 +94,19 @@
         * query_weight[:, :, None]
     )
     attention = (intra_attn + cross_attn).reshape(tok_rows, heads_here * HEAD_DIM)
-    squares = lax.psum(jnp.sum(attention * attention, axis=1), "head")
+    squares = jnp.sum(attention * attention, axis=1)
+    if direct:
+        step = 1
+        while step < head_count:
+            squares += lax.ppermute(squares, "head", [(h, h ^ step) for h in range(head_count)])
+            step *= 2
+    else:
+        squares = lax.psum(squares, "head")
     inv_scale = lax.rsqrt(squares / (heads_here * HEAD_DIM * head_count) + 1e-06)
     gated = attention * norm_gain.astype(f32) * jax.nn.sigmoid(gate_logits.astype(f32))
     contract = (((1,), (1,)), ((), ()))
 
-    if seq_count != head_count:
+    if not direct:
         partials = lax.dot_general(
             (gated * inv_scale[:, None]).astype(jnp.bfloat16),
             lax.all_gather(out_weight, "seq", axis=0, tiled=True),
@@ -96,21 +117,42 @@
         return summed.astype(jnp.bfloat16)
 
     gated = gated.astype(jnp.bfloat16)
-    swap = [
-        (s * head_count + h, h * head_count + s)
-        for s in range(seq_count)
-        for h in range(head_count)
-    ]
+    head = lax.axis_index("head")
+    same = (mine % 2) == (head % 2)
+    pairs = seq_count // 2
     rows = tok_rows // CHUNKS
     pieces = []
     for c in range(CHUNKS):
-        everyone = lax.all_gather(gated[c * rows : (c + 1) * rows], "seq", axis=0, tiled=True)
-        partials = lax.dot_general(everyone, out_weight, contract, preferred_element_type=f32)
-        summed = lax.psum_scatter(
-            partials.astype(jnp.bfloat16), "head", scatter_dimension=0, tiled=True
-        )
-        pieces.append(lax.ppermute(summed, ("seq", "head"), swap))
-    out = jnp.concatenate(pieces, axis=0).astype(f32) * inv_scale[:, None]
+        part = gated[c * rows : (c + 1) * rows]
+        given = [part] + [
+            lax.ppermute(part, "seq", [(s, s ^ k) for s in range(seq_count)])
+            for k in range(1, seq_count)
+        ]
+        reduced = []
+        for p in range(pairs):
+            here, there = given[2 * p], given[2 * p + 1]
+            other = lax.dot_general(
+                jnp.where(same, there, here), out_weight, contract, preferred_element_type=f32
+            ).astype(jnp.bfloat16)
+            came = lax.ppermute(other, "head", [(h, h ^ 1) for h in range(head_count)])
+            kept = lax.dot_general(
+                jnp.where(same, here, there), out_weight, contract, preferred_element_type=f32
+            )
+            reduced.append((kept + came.astype(f32)).astype(jnp.bfloat16))
+        total = jnp.zeros(reduced[0].shape, f32)
+        for j in range(pairs):
+            pick = jnp.bitwise_xor(jnp.bitwise_xor(mine // 2, head // 2), j)
+            chosen = reduced[0]
+            for p in range(1, pairs):
+                chosen = jnp.where(pick == p, reduced[p], chosen)
+            route = [
+                (s * head_count + h, (h ^ (2 * j)) * head_count + s)
+                for s in range(seq_count)
+                for h in range(head_count)
+            ]
+            total += lax.ppermute(chosen, ("seq", "head"), route).astype(f32)
+        pieces.append(total)
+    out = jnp.concatenate(pieces, axis=0) * inv_scale[:, None]
     return out.astype(jnp.bfloat16)
 
 

time: 286 us -> 224 us (0.78)
  waiting for transfers between devices: 209 us -> 102 us
  starting transfers between devices: 10.8 us -> 74.4 us
  between operations: 13.9 us -> 0.94 us
  blocking collectives: 5.56 us -> 0 us
    all_gather x3 -> x0, waiting for transfers between devices: 103 us -> none  [the longest x2 83 us: shards(): lax.all_gather(gated[c * rows:(c + 1) * rows], 'seq', axis=0, tiled=True)]
    reduce_scatter x2 -> x0, waiting for transfers between devices: 77.4 us -> none  [shards(): lax.psum_scatter(partials.astype(jnp.bfloat16), 'head', scatter_dimension...]
    ppermute x2 -> x19, waiting for transfers between devices: 28.1 us -> 102 us  [the longest x4 46.2 us: shards(): total += lax.ppermute(chosen, ('seq', 'head'), route).astype(f32)]
    ppermute x2 -> x19, starting transfers between devices: 10.7 us -> 74.4 us  [the longest x4 46 us: shards(): came = lax.ppermute(other, 'head', [(h, h ^ 1) for h in range(head_count)])]
    psum x1 -> x0, blocking collectives: 5.56 us -> none  [shards(): squares = lax.psum(jnp.sum(attention * attention, axis=1), 'head')]
    dot_general x2 -> x8, matrix products: 12.9 us -> 12.4 us  [the longest x4 6.45 us: shards(): lax.dot_general(jnp.where(same, there, here), out_weight, contract, prefe...]
  transfers between devices with their start and end apart: 7 -> 19, of which waited for: 6 -> 10; matrix products, arithmetic and copies ran while one was open for 8% -> 10% of each run, Pallas kernels for 0% -> 0%
where the time goes in v3:
time: 224 us; the launch traced here: 220 us
  waiting for transfers between devices  102 us (46%)
  starting transfers between devices  74.4 us (33%)
  matrix products  26.2 us (12%)
  other arithmetic  8.73 us (4%)
  local copies, waits for them, and re-layouts  7.82 us (3%)
    ppermute x4, waiting for transfers between devices, shards(): total += lax.ppermute(chosen, ('seq', 'head'), route).astype(f32)  46.2 us
    ppermute x4, starting transfers between devices, shards(): came = lax.ppermute(other, 'head', [(h, h ^ 1) for h in range(head_count)])  46 us
    ppermute x6, waiting for transfers between devices, shards(): lax.ppermute(part, 'seq', [(s, s ^ k) for s in range(seq_count)])  33.8 us
    ppermute x2, waiting for transfers between devices, shards(): lax.ppermute(squares, 'head', [(h, h ^ step) for h in range(head_count)])  11.4 us
    ppermute x3, waiting for transfers between devices, shards(): lax.ppermute(sent_state, 'seq', [(s, s + k) for s in range(seq_count - k)])  10.8 us
    ppermute x4, starting transfers between devices, shards(): total += lax.ppermute(chosen, ('seq', 'head'), route).astype(f32)  8.29 us
    ppermute x6, starting transfers between devices, shards(): lax.ppermute(part, 'seq', [(s, s ^ k) for s in range(seq_count)])  8.13 us
    ppermute x3, starting transfers between devices, shards(): lax.ppermute(sent_state, 'seq', [(s, s + k) for s in range(seq_count - k)])  8.12 us
  transfers between devices with their start and end apart: 19, of which 10 were waited for; matrix products, arithmetic and copies ran while one was open for 10% of the time, Pallas kernels for 0%

profile of v3, /device:TPU:11, one launch (start us, length us, event | category | flops | bytes accessed | tf_op | source)
XLA Modules:
  0.0 220.3 jit_solution(2559467183752966725)
XLA Ops:
  3.1 2.3 %copy.22 = bf16[512,1024]{0,1:T(8,128)(2,1)} copy(bf16[512,1024]{1,0:T(8,128)(2,1)} %param.9) | data formatting | bytes 2097152 | tf_op jit(solution)/shard_map/reshape | solution.py:38
  5.5 2.7 %convolution_convert_fusion.4 = bf16[8,128,128]{2,1,0:T(8,128)(2,1)} fusion(bf16[512,8,128]{0,2,1:T(8,128)(2,1)} %bitcast.53, f32[512,8]{0,1:T(8,128)S(1)} %get-tuple-element.18, bf16[512,1024]{1,0:T(8,128)(2,1)} %param.10), kind=kOutput, calls=%fused_computation.28 | convolution fusion | flops 135921664 | bytes 2375680 | tf_op jit(solution)/shard_map/thd,the->hde/dot_general | solution.py:47
  8.8 5.5 %collective-permute-start.1 = (bf16[8,128,128]{2,1,0:T(8,128)(2,1)}, bf16[8,128,128]{2,1,0:T(8,128)(2,1)}, u32[]{:S(2)}, u32[]{:S(2)}) collective-permute-start(bf16[8,128,128]{2,1,0:T(8,128)(2,1)} %convolution_convert_fusion.4), channel_id=1, source_target_pairs={{0,8},{4,12},{1,9},{5,13},{2,10},{6,14},{3,11},{7,15},{16,24},{20,... | collective-permute-start | bytes 786440 | tf_op jit(solution)/shard_map/ppermute | solution.py:52
  14.4 1.9 collective-permute-start
  18.8 6.9 %fusion = f32[8,512,128]{1,2,0:T(8,128)} fusion(f32[512,512]{1,0:T(8,128)} %fusion.19, f32[8]{0:T(128)S(1)} %get-tuple-element.6, pred[512,512]{1,0:T(8,128)(4,1)} %fusion.22, bf16[512,8,128]{0,2,1:T(8,128)(2,1)} %bitcast.54, bf16[512,1024]{1,0:T(8,128)(2,1)} %param.10, bf16[512,1024]{1,0:T(8,128)(2,1)} %param.8), kind=kOutput, calls=%fused_computation.1 | convolution fusion | flops 1082130432 | bytes 6553632 | tf_op jit(solution)/shard_map/hts,shd->thd/dot_general | solution.py:74
  25.8 5.1 %collective-permute-done.1 = bf16[8,128,128]{2,1,0:T(8,128)(2,1)} collective-permute-done((bf16[8,128,128]{2,1,0:T(8,128)(2,1)}, bf16[8,128,128]{2,1,0:T(8,128)(2,1)}, u32[]{:S(2)}, u32[]{:S(2)}) %collective-permute-start.1) | collective-permute-done | bytes 262176 | tf_op jit(solution)/shard_map/ppermute | solution.py:52
  30.9 5.6 %collective-permute-done = bf16[8,128,128]{2,1,0:T(8,128)(2,1)} collective-permute-done((bf16[8,128,128]{2,1,0:T(8,128)(2,1)}, bf16[8,128,128]{2,1,0:T(8,128)(2,1)}, u32[]{:S(2)}, u32[]{:S(2)}) %collective-permute-start) | collective-permute-done | bytes 262176 | tf_op jit(solution)/shard_map/ppermute | solution.py:52
  36.5 4.3 %multiply_reduce_fusion = (f32[512]{0:T(512)S(1)}, f32[512,8,128]{0,2,1:T(8,128)}) fusion(f32[512,8]{0,1:T(8,128)S(1)} %get-tuple-element.19, bf16[8,128,128]{2,1,0:T(8,128)(2,1)S(1)} %collective-permute-done.2, bf16[8,128,128]{2,1,0:T(8,128)(2,1)} %collective-permute-done.1, bf16[8,128,128]{2,1,0:T(8,128)(2,1)} %collective-permute-done, ...), kind=kOutput, calls=%fused_computation.23 | convolution fusion | flops 137494016 | bytes 6047840 | tf_op jit(solution)/shard_map/thd,hde->the/dot_general | solution.py:88
  40.8 2.9 %copy.20 = f32[512,1024]{1,0:T(8,128)} copy(f32[512,1024]{0,1:T(8,128)} %bitcast.52) | data formatting | bytes 4194304 | tf_op jit(solution)/shard_map/reshape | solution.py:96
  43.7 2.5 %multiply_convert_fusion.2 = bf16[512,1024]{1,0:T(8,128)(2,1)S(1)} fusion(bf16[512,1024]{1,0:T(8,128)(2,1)} %param.11, f32[512,1024]{1,0:T(8,128)} %copy.20, f32[1024]{0:T(1024)S(1)} %convert_element_type.123), kind=kLoop, calls=%fused_computation.24 | loop fusion | flops 3670016 | bytes 4198400 | tf_op jit(solution)/shard_map/convert_element_type | solution.py:119
  48.2 2.2 collective-permute-start.11
  50.4 1.3 collective-permute-start.10
  54.0 7.6 %collective-permute-done.13 = bf16[256,1024]{1,0:T(8,128)(2,1)} collective-permute-done((bf16[256,1024]{1,0:T(8,128)(2,1)}, bf16[256,1024]{1,0:T(8,128)(2,1)}, u32[]{:S(2)}, u32[]{:S(2)}) %collective-permute-start.13) | collective-permute-done | bytes 524320 | tf_op jit(solution)/shard_map/ppermute | solution.py:128
  61.5 2.4 %collective-permute-start.3 = (bf16[256,1024]{1,0:T(8,128)(2,1)}, bf16[256,1024]{1,0:T(8,128)(2,1)S(1)}, u32[]{:S(2)}, u32[]{:S(2)}) collective-permute-start(bf16[256,1024]{1,0:T(8,128)(2,1)} %get-tuple-element.13), channel_id=1, source_target_pairs={{0,8},{4,12},{8,0},{12,4},{1,9},{5,13},{9,1},{13,5},{2,10},{6,14},... | collective-permute-start | bytes 1572872 | tf_op jit(solution)/shard_map/ppermute | solution.py:128
  63.9 2.2 %convolution_convert_fusion = bf16[256,1536]{1,0:T(8,128)(2,1)S(1)} fusion(bf16[1536,1024]{1,0:T(8,128)(2,1)S(1)} %copy-done, bf16[256,1024]{1,0:T(8,128)(2,1)} %collective-permute-done.13, pred[]{:T(512)S(6)} %eq.15, bf16[512,1024]{1,0:T(8,128)(2,1)} %copy-done.1), kind=kOutput, calls=%fused_computation.17 | convolution fusion | flops 805961728 | bytes 4980737 | tf_op jit(solution)/shard_map/dot_general | solution.py:134
  66.2 20.1 %collective-permute-start.14 = (bf16[256,1536]{1,0:T(8,128)(2,1)S(1)}, bf16[256,1536]{1,0:T(8,128)(2,1)S(1)}, u32[]{:S(2)}, u32[]{:S(2)}) collective-permute-start(bf16[256,1536]{1,0:T(8,128)(2,1)S(1)} %convolution_convert_fusion), channel_id=1, source_target_pairs={{0,1},{1,0},{2,3},{3,2},{4,5},{5,4},{6,7},{7,6},{8,9},{9,8},{10,11... | collective-permute-start | bytes 2359304 | tf_op jit(solution)/shard_map/ppermute | solution.py:137
  86.3 9.4 %collective-permute-done.10 = bf16[256,1024]{1,0:T(8,128)(2,1)} collective-permute-done((bf16[256,1024]{1,0:T(8,128)(2,1)}, bf16[256,1024]{1,0:T(8,128)(2,1)}, u32[]{:S(2)}, u32[]{:S(2)}) %collective-permute-start.10) | collective-permute-done | bytes 524320 | tf_op jit(solution)/shard_map/ppermute | solution.py:128
  95.7 2.1 convolution_convert_fusion.1
  97.8 24.4 %collective-permute-start.12 = (bf16[256,1536]{1,0:T(8,128)(2,1)S(1)}, bf16[256,1536]{1,0:T(8,128)(2,1)S(1)}, u32[]{:S(2)}, u32[]{:S(2)}) collective-permute-start(bf16[256,1536]{1,0:T(8,128)(2,1)S(1)} %convolution_convert_fusion.1), channel_id=1, source_target_pairs={{0,1},{1,0},{2,3},{3,2},{4,5},{5,4},{6,7},{7,6},{8,9},{9,8},{10,11... | collective-permute-start | bytes 2359304 | tf_op jit(solution)/shard_map/ppermute | solution.py:137
  123.3 6.6 %collective-permute-done.4 = bf16[256,1024]{1,0:T(8,128)(2,1)S(1)} collective-permute-done((bf16[256,1024]{1,0:T(8,128)(2,1)}, bf16[256,1024]{1,0:T(8,128)(2,1)S(1)}, u32[]{:S(2)}, u32[]{:S(2)}) %collective-permute-start.4) | collective-permute-done | bytes 524320 | tf_op jit(solution)/shard_map/ppermute | solution.py:128
  129.9 10.2 %collective-permute-done.3 = bf16[256,1024]{1,0:T(8,128)(2,1)S(1)} collective-permute-done((bf16[256,1024]{1,0:T(8,128)(2,1)}, bf16[256,1024]{1,0:T(8,128)(2,1)S(1)}, u32[]{:S(2)}, u32[]{:S(2)}) %collective-permute-start.3) | collective-permute-done | bytes 524320 | tf_op jit(solution)/shard_map/ppermute | solution.py:128
  141.3 1.4 collective-permute-start.5
  143.8 2.4 %broadcast_select_fusion.2 = (bf16[256,1536]{1,0:T(8,128)(2,1)S(1)}, bf16[256,1536]{1,0:T(8,128)(2,1)S(1)}) fusion(bf16[256,1536]{1,0:T(8,128)(2,1)S(1)} %fusion.11, pred[]{:T(512)S(6)} %eq.14, pred[]{:T(512)S(6)} %eq.16, bf16[256,1536]{1,0:T(8,128)(2,1)S(1)} %collective-permute-done.12, bf16[1536,1024]{1,0:T(8,128)(2,1)S(1)} %copy-done, ...), kind=kOutput, calls=%fused_computation.45 | convolution fusion | flops 807534592 | bytes 7340035 | tf_op jit(solution)/shard_map/dot_general | solution.py:138
  146.4 6.0 %collective-permute-start.15 = (bf16[256,1536]{1,0:T(8,128)(2,1)S(1)}, bf16[256,1536]{1,0:T(8,128)(2,1)S(1)}, u32[]{:S(2)}, u32[]{:S(2)}) collective-permute-start(bf16[256,1536]{1,0:T(8,128)(2,1)S(1)} %get-tuple-element.11), channel_id=1, source_target_pairs={{0,0},{1,4},{2,8},{3,12},{4,1},{5,5},{6,9},{7,13},{8,2},{9,6},{10,... | collective-permute-start | bytes 2359304 | tf_op jit(solution)/shard_map/ppermute | solution.py:153
  153.6 1.4 broadcast_select_fusion.3
  155.0 1.9 collective-permute-start.8
  157.0 2.7 %collective-permute-start.17 = (f32[512]{0:T(512)S(1)}, f32[512]{0:T(512)S(1)}, u32[]{:S(2)}, u32[]{:S(2)}) collective-permute-start(f32[512]{0:T(512)S(1)} %get-tuple-element.20), channel_id=1, source_target_pairs={{0,1},{1,0},{2,3},{3,2},{4,5},{5,4},{6,7},{7,6},{8,9},{9,8},{10,11... | collective-permute-start | bytes 6152 | tf_op jit(solution)/shard_map/ppermute | solution.py:101
  160.5 1.2 collective-permute-start.18
  161.7 10.6 %collective-permute-done.18 = f32[512]{0:T(512)S(1)} collective-permute-done((f32[512]{0:T(512)S(1)}, f32[512]{0:T(512)S(1)}, u32[]{:S(2)}, u32[]{:S(2)}) %collective-permute-start.18) | collective-permute-done | bytes 2080 | tf_op jit(solution)/shard_map/ppermute | solution.py:101
  172.3 29.6 %collective-permute-done.15 = bf16[256,1536]{1,0:T(8,128)(2,1)S(1)} collective-permute-done((bf16[256,1536]{1,0:T(8,128)(2,1)S(1)}, bf16[256,1536]{1,0:T(8,128)(2,1)S(1)}, u32[]{:S(2)}, u32[]{:S(2)}) %collective-permute-start.15) | collective-permute-done | bytes 786464 | tf_op jit(solution)/shard_map/ppermute | solution.py:153
  202.1 16.6 %collective-permute-done.8 = bf16[256,1536]{1,0:T(8,128)(2,1)S(1)} collective-permute-done((bf16[256,1536]{1,0:T(8,128)(2,1)S(1)}, bf16[256,1536]{1,0:T(8,128)(2,1)S(1)}, u32[]{:S(2)}, u32[]{:S(2)}) %collective-permute-start.8) | collective-permute-done | bytes 786464 | tf_op jit(solution)/shard_map/ppermute | solution.py:153
  219.0 1.4 fusion.7
  (55 shorter events, 16.0 us)
Async XLA Ops:
  0.0 63.9 %copy-start = (bf16[1536,1024]{1,0:T(8,128)(2,1)S(1)}, bf16[1536,1024]{1,0:T(8,128)(2,1)}, u32[]{:S(2)}) copy-start(bf16[1536,1024]{1,0:T(8,128)(2,1)} %param.15) | copy-start | bytes 9437188
  5.4 13.2 %copy-start.3 = (bf16[1024]{0:T(1024)(128)(2,1)S(1)}, bf16[1024]{0:T(1024)(128)(2,1)}, u32[]{:S(2)}) copy-start(bf16[1024]{0:T(1024)(128)(2,1)} %param.12) | copy-start | bytes 6148
  8.2 17.6 %collective-permute-start.2 = (bf16[8,128,128]{2,1,0:T(8,128)(2,1)}, bf16[8,128,128]{2,1,0:T(8,128)(2,1)S(1)}, u32[]{:S(2)}, u32[]{:S(2)}) collective-permute-start(bf16[8,128,128]{2,1,0:T(8,128)(2,1)} %convolution_convert_fusion.4), channel_id=1, source_target_pairs={{0,12},{1,13},{2,14},{3,15},{16,28},{17,29},{18,30},{19,31}} | collective-permute-start | bytes 786440 | tf_op jit(solution)/shard_map/ppermute | solution.py:52
  8.8 22.0 %collective-permute-start.1 = (bf16[8,128,128]{2,1,0:T(8,128)(2,1)}, bf16[8,128,128]{2,1,0:T(8,128)(2,1)}, u32[]{:S(2)}, u32[]{:S(2)}) collective-permute-start(bf16[8,128,128]{2,1,0:T(8,128)(2,1)} %convolution_convert_fusion.4), channel_id=1, source_target_pairs={{0,8},{4,12},{1,9},{5,13},{2,10},{6,14},{3,11},{7,15},{16,24},{20,... | collective-permute-start | bytes 786440 | tf_op jit(solution)/shard_map/ppermute | solution.py:52
  14.4 22.1 %collective-permute-start = (bf16[8,128,128]{2,1,0:T(8,128)(2,1)}, bf16[8,128,128]{2,1,0:T(8,128)(2,1)}, u32[]{:S(2)}, u32[]{:S(2)}) collective-permute-start(bf16[8,128,128]{2,1,0:T(8,128)(2,1)} %convolution_convert_fusion.4), channel_id=1, source_target_pairs={{0,4},{4,8},{8,12},{1,5},{5,9},{9,13},{2,6},{6,10},{10,14},{3,7},{... | collective-permute-start | bytes 786440 | tf_op jit(solution)/shard_map/ppermute | solution.py:52
  46.2 1.0 copy-start.1
  48.2 13.3 %collective-permute-start.13 = (bf16[256,1024]{1,0:T(8,128)(2,1)}, bf16[256,1024]{1,0:T(8,128)(2,1)}, u32[]{:S(2)}, u32[]{:S(2)}) collective-permute-start(bf16[256,1024]{1,0:T(8,128)(2,1)} %get-tuple-element.14), channel_id=1, source_target_pairs={{0,4},{4,0},{8,12},{12,8},{1,5},{5,1},{9,13},{13,9},{2,6},{6,2},{1... | collective-permute-start | bytes 1572872 | tf_op jit(solution)/shard_map/ppermute | solution.py:128
  48.2 17.9 %collective-permute-start.11 = (bf16[256,1024]{1,0:T(8,128)(2,1)}, bf16[256,1024]{1,0:T(8,128)(2,1)}, u32[]{:S(2)}, u32[]{:S(2)}) collective-permute-start(bf16[256,1024]{1,0:T(8,128)(2,1)} %get-tuple-element.14), channel_id=1, source_target_pairs={{0,12},{4,8},{8,4},{12,0},{1,13},{5,9},{9,5},{13,1},{2,14},{6,10},... | collective-permute-start | bytes 1572872 | tf_op jit(solution)/shard_map/ppermute | solution.py:128
  50.4 45.3 %collective-permute-start.10 = (bf16[256,1024]{1,0:T(8,128)(2,1)}, bf16[256,1024]{1,0:T(8,128)(2,1)}, u32[]{:S(2)}, u32[]{:S(2)}) collective-permute-start(bf16[256,1024]{1,0:T(8,128)(2,1)} %get-tuple-element.14), channel_id=1, source_target_pairs={{0,8},{4,12},{8,0},{12,4},{1,9},{5,13},{9,1},{13,5},{2,10},{6,14},... | collective-permute-start | bytes 1572872 | tf_op jit(solution)/shard_map/ppermute | solution.py:128
  51.8 70.4 %collective-permute-start.6 = (bf16[256,1024]{1,0:T(8,128)(2,1)}, bf16[256,1024]{1,0:T(8,128)(2,1)S(1)}, u32[]{:S(2)}, u32[]{:S(2)}) collective-permute-start(bf16[256,1024]{1,0:T(8,128)(2,1)} %get-tuple-element.13), channel_id=1, source_target_pairs={{0,4},{4,0},{8,12},{12,8},{1,5},{5,1},{9,13},{13,9},{2,6},{6,2},{1... | collective-permute-start | bytes 1572872 | tf_op jit(solution)/shard_map/ppermute | solution.py:128
  52.8 77.1 %collective-permute-start.4 = (bf16[256,1024]{1,0:T(8,128)(2,1)}, bf16[256,1024]{1,0:T(8,128)(2,1)S(1)}, u32[]{:S(2)}, u32[]{:S(2)}) collective-permute-start(bf16[256,1024]{1,0:T(8,128)(2,1)} %get-tuple-element.13), channel_id=1, source_target_pairs={{0,12},{4,8},{8,4},{12,0},{1,13},{5,9},{9,5},{13,1},{2,14},{6,10},... | collective-permute-start | bytes 1572872 | tf_op jit(solution)/shard_map/ppermute | solution.py:128
  61.5 78.6 %collective-permute-start.3 = (bf16[256,1024]{1,0:T(8,128)(2,1)}, bf16[256,1024]{1,0:T(8,128)(2,1)S(1)}, u32[]{:S(2)}, u32[]{:S(2)}) collective-permute-start(bf16[256,1024]{1,0:T(8,128)(2,1)} %get-tuple-element.13), channel_id=1, source_target_pairs={{0,8},{4,12},{8,0},{12,4},{1,9},{5,13},{9,1},{13,5},{2,10},{6,14},... | collective-permute-start | bytes 1572872 | tf_op jit(solution)/shard_map/ppermute | solution.py:128
  66.1 56.0 %copy-start.2 = (bf16[512,1024]{1,0:T(8,128)(2,1)S(1)}, bf16[512,1024]{1,0:T(8,128)(2,1)}, u32[]{:S(2)}) copy-start(bf16[512,1024]{1,0:T(8,128)(2,1)} %copy-done.1) | copy-start | bytes 3145732
  66.2 76.5 %collective-permute-start.14 = (bf16[256,1536]{1,0:T(8,128)(2,1)S(1)}, bf16[256,1536]{1,0:T(8,128)(2,1)S(1)}, u32[]{:S(2)}, u32[]{:S(2)}) collective-permute-start(bf16[256,1536]{1,0:T(8,128)(2,1)S(1)} %convolution_convert_fusion), channel_id=1, source_target_pairs={{0,1},{1,0},{2,3},{3,2},{4,5},{5,4},{6,7},{7,6},{8,9},{9,8},{10,11... | collective-permute-start | bytes 2359304 | tf_op jit(solution)/shard_map/ppermute | solution.py:137
  97.8 46.0 %collective-permute-start.12 = (bf16[256,1536]{1,0:T(8,128)(2,1)S(1)}, bf16[256,1536]{1,0:T(8,128)(2,1)S(1)}, u32[]{:S(2)}, u32[]{:S(2)}) collective-permute-start(bf16[256,1536]{1,0:T(8,128)(2,1)S(1)} %convolution_convert_fusion.1), channel_id=1, source_target_pairs={{0,1},{1,0},{2,3},{3,2},{4,5},{5,4},{6,7},{7,6},{8,9},{9,8},{10,11... | collective-permute-start | bytes 2359304 | tf_op jit(solution)/shard_map/ppermute | solution.py:137
  123.2 29.2 %collective-permute-start.7 = (bf16[256,1536]{1,0:T(8,128)(2,1)S(1)}, bf16[256,1536]{1,0:T(8,128)(2,1)S(1)}, u32[]{:S(2)}, u32[]{:S(2)}) collective-permute-start(bf16[256,1536]{1,0:T(8,128)(2,1)S(1)} %convolution_convert_fusion.2), channel_id=1, source_target_pairs={{0,1},{1,0},{2,3},{3,2},{4,5},{5,4},{6,7},{7,6},{8,9},{9,8},{10,11... | collective-permute-start | bytes 2359304 | tf_op jit(solution)/shard_map/ppermute | solution.py:137
  141.3 12.3 %collective-permute-start.5 = (bf16[256,1536]{1,0:T(8,128)(2,1)S(1)}, bf16[256,1536]{1,0:T(8,128)(2,1)S(1)}, u32[]{:S(2)}, u32[]{:S(2)}) collective-permute-start(bf16[256,1536]{1,0:T(8,128)(2,1)S(1)} %convolution_convert_fusion.3), channel_id=1, source_target_pairs={{0,1},{1,0},{2,3},{3,2},{4,5},{5,4},{6,7},{7,6},{8,9},{9,8},{10,11... | collective-permute-start | bytes 2359304 | tf_op jit(solution)/shard_map/ppermute | solution.py:137
  146.1 26.1 %collective-permute-start.16 = (bf16[256,1536]{1,0:T(8,128)(2,1)S(1)}, bf16[256,1536]{1,0:T(8,128)(2,1)S(1)}, u32[]{:S(2)}, u32[]{:S(2)}) collective-permute-start(bf16[256,1536]{1,0:T(8,128)(2,1)S(1)} %get-tuple-element.12), channel_id=1, source_target_pairs={{0,8},{1,12},{2,0},{3,4},{4,9},{5,13},{6,1},{7,5},{8,10},{9,14},{1... | collective-permute-start | bytes 2359304 | tf_op jit(solution)/shard_map/ppermute | solution.py:153
  146.4 55.4 %collective-permute-start.15 = (bf16[256,1536]{1,0:T(8,128)(2,1)S(1)}, bf16[256,1536]{1,0:T(8,128)(2,1)S(1)}, u32[]{:S(2)}, u32[]{:S(2)}) collective-permute-start(bf16[256,1536]{1,0:T(8,128)(2,1)S(1)} %get-tuple-element.11), channel_id=1, source_target_pairs={{0,0},{1,4},{2,8},{3,12},{4,1},{5,5},{6,9},{7,13},{8,2},{9,6},{10,... | collective-permute-start | bytes 2359304 | tf_op jit(solution)/shard_map/ppermute | solution.py:153
  155.0 47.1 %collective-permute-start.9 = (bf16[256,1536]{1,0:T(8,128)(2,1)S(1)}, bf16[256,1536]{1,0:T(8,128)(2,1)S(1)}, u32[]{:S(2)}, u32[]{:S(2)}) collective-permute-start(bf16[256,1536]{1,0:T(8,128)(2,1)S(1)} %get-tuple-element.10), channel_id=1, source_target_pairs={{0,8},{1,12},{2,0},{3,4},{4,9},{5,13},{6,1},{7,5},{8,10},{9,14},{1... | collective-permute-start | bytes 2359304 | tf_op jit(solution)/shard_map/ppermute | solution.py:153
  155.0 63.7 %collective-permute-start.8 = (bf16[256,1536]{1,0:T(8,128)(2,1)S(1)}, bf16[256,1536]{1,0:T(8,128)(2,1)S(1)}, u32[]{:S(2)}, u32[]{:S(2)}) collective-permute-start(bf16[256,1536]{1,0:T(8,128)(2,1)S(1)} %get-tuple-element.9), channel_id=1, source_target_pairs={{0,0},{1,4},{2,8},{3,12},{4,1},{5,5},{6,9},{7,13},{8,2},{9,6},{10,... | collective-permute-start | bytes 2359304 | tf_op jit(solution)/shard_map/ppermute | solution.py:153
  157.0 3.5 %collective-permute-start.17 = (f32[512]{0:T(512)S(1)}, f32[512]{0:T(512)S(1)}, u32[]{:S(2)}, u32[]{:S(2)}) collective-permute-start(f32[512]{0:T(512)S(1)} %get-tuple-element.20), channel_id=1, source_target_pairs={{0,1},{1,0},{2,3},{3,2},{4,5},{5,4},{6,7},{7,6},{8,9},{9,8},{10,11... | collective-permute-start | bytes 6152 | tf_op jit(solution)/shard_map/ppermute | solution.py:101
  160.5 11.8 %collective-permute-start.18 = (f32[512]{0:T(512)S(1)}, f32[512]{0:T(512)S(1)}, u32[]{:S(2)}, u32[]{:S(2)}) collective-permute-start(f32[512]{0:T(512)S(1)} %add.112), channel_id=1, source_target_pairs={{0,2},{1,3},{2,0},{3,1},{4,6},{5,7},{6,4},{7,5},{8,10},{9,11},{10,... | collective-permute-start | bytes 6152 | tf_op jit(solution)/shard_map/ppermute | solution.py:101

commit v4 on v3

--- a/solution.py
+++ b/solution.py
@@ -1,10 +1,203 @@
+import functools
+
 import jax
 import jax.numpy as jnp
 from jax import lax
+from jax.experimental import pallas as pl
+from jax.experimental.pallas import tpu as pltpu
 from jax.sharding import PartitionSpec as P
 
 HEAD_DIM = 128
-CHUNKS = 2
+CHUNKS = 4
+
+MESH = pl.DeviceIdType.MESH
+
+
+def project_kernel(
+    count, g_ref, w_ref, out_ref, given, send0, recv0, send1, recv1, hold, send2,
+    hop_send, hop_recv, pair_send, pair_recv, swap_send, swap_recv,
+):
+    me, head = lax.axis_index("seq"), lax.axis_index("head")
+    core, across = head % 2, head // 2
+    mate = head + 1 - 2 * core
+    far = (1 - across) * 2 + core
+    rows = g_ref.shape[0] // CHUNKS
+    width = w_ref.shape[0]
+    tile = width // 3 if width % 384 == 0 else width
+
+    barrier = pltpu.get_barrier_semaphore()
+
+    def greet(**where):
+        pl.semaphore_signal(barrier, inc=1, device_id=where, device_id_type=MESH)
+
+    greet(head=mate)
+    greet(head=far)
+    pl.when(me > 0)(lambda: greet(seq=me - 1))
+    pl.when(me < count - 1)(lambda: greet(seq=me + 1))
+    pl.when(me != head)(lambda: greet(seq=head, head=me))
+    apart, square = (me - head) * (me - head), count * count
+    before, after = (me + count - 1) // count, (2 * count - 2 - me) // count
+    pl.semaphore_wait(barrier, 2 + before + after + (apart + square - 1) // square)
+
+    def hop(way, k, c):
+        block = me - (k - 1) if way == 0 else me + (k - 1)
+        part = pl.ds(c * rows, rows)
+        src = g_ref.at[part] if k == 1 else given.at[block, part]
+        return pltpu.make_async_remote_copy(
+            src_ref=src,
+            dst_ref=given.at[block, part],
+            send_sem=hop_send.at[way, k - 1, c],
+            recv_sem=hop_recv.at[way, k - 1, c],
+            device_id={"seq": me + 1 if way == 0 else me - 1},
+            device_id_type=MESH,
+        )
+
+    def arrival(way, k, c):
+        block = me - k if way == 0 else me + k
+        part = pl.ds(c * rows, rows)
+        return pltpu.make_async_remote_copy(
+            src_ref=given.at[block, part],
+            dst_ref=given.at[block, part],
+            send_sem=hop_send.at[way, k - 1, c],
+            recv_sem=hop_recv.at[way, k - 1, c],
+            device_id={"seq": me + 1 if way == 0 else me - 1},
+            device_id_type=MESH,
+        )
+
+    def sends(way, k):
+        if way == 0:
+            return (me >= k - 1) & (me < count - 1)
+        return (me <= count - k) & (me > 0)
+
+    def comes(way, k):
+        return me >= k if way == 0 else me < count - k
+
+    def start_hop(k, c):
+        for way in (0, 1):
+            pl.when(sends(way, k))(lambda way=way: hop(way, k, c).start())
+
+    def pair_copy(stage, slot, c):
+        src, dst, to = (send1, recv1, far) if stage else (send0, recv0, mate)
+        src, dst = (src.at[c], dst.at[c]) if stage else (src.at[c, slot], dst.at[c, slot])
+        lane = 2 if stage else slot
+        return pltpu.make_async_remote_copy(
+            src_ref=src, dst_ref=dst,
+            send_sem=pair_send.at[lane, c], recv_sem=pair_recv.at[lane, c],
+            device_id={"head": to}, device_id_type=MESH,
+        )
+
+    def swap_copy(c):
+        return pltpu.make_async_remote_copy(
+            src_ref=send2.at[c], dst_ref=out_ref.at[pl.ds(c * rows, rows)],
+            send_sem=swap_send.at[c], recv_sem=swap_recv.at[c],
+            device_id={"seq": head, "head": me}, device_id_type=MESH,
+        )
+
+    def product(block, c, put):
+        @pl.loop(0, width // tile)
+        def _(i):
+            span = pl.ds(pl.multiple_of(i * tile, 128), tile)
+            put(span, lax.dot_general(
+                given[block, pl.ds(c * rows, rows), :], w_ref[span, :],
+                (((1,), (1,)), ((), ())), preferred_element_type=jnp.float32,
+            ))
+
+    def finish(c):
+        pair_copy(1, 0, c).wait_recv()
+        send2[c] = (hold[c] + recv1[c].astype(jnp.float32)).astype(jnp.bfloat16)
+
+        @pl.when(me != head)
+        def _():
+            swap_copy(c).start()
+
+        @pl.when(me == head)
+        def _():
+            out_ref[pl.ds(c * rows, rows), :] = send2[c]
+
+    start_hop(1, 0)
+    start_hop(1, 1)
+    given[me] = g_ref[...]
+    for c in range(CHUNKS):
+        for k in range(1, count):
+            for way in (0, 1):
+                pl.when(comes(way, k))(lambda way=way: arrival(way, k, c).wait_recv())
+            if k < count - 1:
+                start_hop(k + 1, c)
+        if c + 2 < CHUNKS:
+            start_hop(1, c + 2)
+
+        for slot in range(2):
+            def put_other(span, value):
+                send0[c, slot, :, span] = value.astype(jnp.bfloat16)
+
+            side = 1 - across if slot == 0 else across
+            product(2 * side + 1 - core, c, put_other)
+            pair_copy(0, slot, c).start()
+
+        pair_copy(0, 0, c).wait_recv()
+
+        def put_far(span, value):
+            total = value + recv0[c, 0, :, span].astype(jnp.float32)
+            send1[c, :, span] = total.astype(jnp.bfloat16)
+
+        product(far, c, put_far)
+        pair_copy(1, 0, c).start()
+        pair_copy(0, 1, c).wait_recv()
+
+        def put_mine(span, value):
+            hold[c, :, span] = value + recv0[c, 1, :, span].astype(jnp.float32)
+
+        product(head, c, put_mine)
+        if c > 0:
+            finish(c - 1)
+    finish(CHUNKS - 1)
+    for c in range(CHUNKS):
+        for k in range(1, count):
+            for way in (0, 1):
+                pl.when(sends(way, k))(lambda way=way: hop(way, k, c).wait_send())
+        for slot in range(2):
+            pair_copy(0, slot, c).wait_send()
+        pair_copy(1, 0, c).wait_send()
+
+        @pl.when(me != head)
+        def _():
+            swap_copy(c).wait()
+
+
+def project(gated, out_weight, count):
+    tok_rows, depth = gated.shape
+    width = out_weight.shape[0]
+    rows = tok_rows // CHUNKS
+    half = functools.partial(pltpu.VMEM, dtype=jnp.bfloat16)
+    return pl.pallas_call(
+        functools.partial(project_kernel, count),
+        out_shape=jax.ShapeDtypeStruct((tok_rows, width), jnp.bfloat16),
+        in_specs=[pl.BlockSpec(memory_space=pltpu.VMEM)] * 2,
+        out_specs=pl.BlockSpec(memory_space=pltpu.VMEM),
+        scratch_shapes=[
+            half((count, tok_rows, depth)),
+            half((CHUNKS, 2, rows, width)),
+            half((CHUNKS, 2, rows, width)),
+            half((CHUNKS, rows, width)),
+            half((CHUNKS, rows, width)),
+            pltpu.VMEM((CHUNKS, rows, width), jnp.float32),
+            half((CHUNKS, rows, width)),
+            pltpu.SemaphoreType.DMA((2, count - 1, CHUNKS)),
+            pltpu.SemaphoreType.DMA((2, count - 1, CHUNKS)),
+            pltpu.SemaphoreType.DMA((3, CHUNKS)),
+            pltpu.SemaphoreType.DMA((3, CHUNKS)),
+            pltpu.SemaphoreType.DMA((CHUNKS,)),
+            pltpu.SemaphoreType.DMA((CHUNKS,)),
+        ],
+        compiler_params=pltpu.CompilerParams(
+            collective_id=0, has_side_effects=True, vmem_limit_bytes=48 * 1024 * 1024
+        ),
+        cost_estimate=pl.CostEstimate(
+            flops=2 * count * tok_rows * depth * width,
+            bytes_accessed=2 * (tok_rows * depth + width * depth + tok_rows * width),
+            transcendentals=0,
+        ),
+    )(gated, out_weight)
 
 
 def doc_positions(doc_lengths, position):
@@ -45,7 +238,7 @@
     )
     scaled = (key_heads.astype(f32) * key_weight[:, :, None]).astype(jnp.bfloat16)
     block_state = jnp.einsum("thd,the->hde", scaled, value_heads, preferred_element_type=f32)
-    direct = seq_count == head_count and head_count & (head_count - 1) == 0 and head_count > 1
+    direct = seq_count == head_count and head_count // 2 == 2 and head_count % 2 == 0
     sent_state = block_state.astype(jnp.bfloat16)
     if direct:
         states = [
@@ -117,42 +310,7 @@
         return summed.astype(jnp.bfloat16)
 
     gated = gated.astype(jnp.bfloat16)
-    head = lax.axis_index("head")
-    same = (mine % 2) == (head % 2)
-    pairs = seq_count // 2
-    rows = tok_rows // CHUNKS
-    pieces = []
-    for c in range(CHUNKS):
-        part = gated[c * rows : (c + 1) * rows]
-        given = [part] + [
-            lax.ppermute(part, "seq", [(s, s ^ k) for s in range(seq_count)])
-            for k in range(1, seq_count)
-        ]
-        reduced = []
-        for p in range(pairs):
-            here, there = given[2 * p], given[2 * p + 1]
-            other = lax.dot_general(
-                jnp.where(same, there, here), out_weight, contract, preferred_element_type=f32
-            ).astype(jnp.bfloat16)
-            came = lax.ppermute(other, "head", [(h, h ^ 1) for h in range(head_count)])
-            kept = lax.dot_general(
-                jnp.where(same, here, there), out_weight, contract, preferred_element_type=f32
-            )
-            reduced.append((kept + came.astype(f32)).astype(jnp.bfloat16))
-        total = jnp.zeros(reduced[0].shape, f32)
-        for j in range(pairs):
-            pick = jnp.bitwise_xor(jnp.bitwise_xor(mine // 2, head // 2), j)
-            chosen = reduced[0]
-            for p in range(1, pairs):
-                chosen = jnp.where(pick == p, reduced[p], chosen)
-            route = [
-                (s * head_count + h, (h ^ (2 * j)) * head_count + s)
-                for s in range(seq_count)
-                for h in range(head_count)
-            ]
-            total += lax.ppermute(chosen, ("seq", "head"), route).astype(f32)
-        pieces.append(total)
-    out = jnp.concatenate(pieces, axis=0) * inv_scale[:, None]
+    out = project(gated, out_weight, seq_count).astype(f32) * inv_scale[:, None]
     return out.astype(jnp.bfloat16)
 
 

time: 224 us -> 178 us (0.79)
  Pallas kernels: 0 us -> 135 us
  waiting for transfers between devices: 102 us -> 9.91 us
  starting transfers between devices: 74.4 us -> 9.47 us
  matrix products: 26.2 us -> 9.61 us
  local copies, waits for them, and re-layouts: 7.82 us -> 4.02 us
    pallas_call x0 -> x1, Pallas kernels: none -> 135 us  [project(): pl.pallas_call(functools.partial(project_kernel, count), out_shape=jax.Sh...]
    ppermute x14 -> x0, waiting for transfers between devices: 80 us -> none  [the longest x4 46.2 us: shards(): total += lax.ppermute(chosen, ('seq', 'head'), route).astype(f32)]
    ppermute x14 -> x0, starting transfers between devices: 62.4 us -> none  [the longest x4 46 us: shards(): came = lax.ppermute(other, 'head', [(h, h ^ 1) for h in range(head_count)])]
    dot_general x8 -> x0, matrix products: 12.4 us -> none  [the longest x4 6.45 us: shards(): lax.dot_general(jnp.where(same, there, here), out_weight, contract, prefe...]
    ppermute x2, waiting for transfers between devices: 11.4 us -> 0.01 us  [shards(): lax.ppermute(squares, 'head', [(h, h ^ step) for h in range(head_count)])]
  transfers between devices with their start and end apart: 19 -> 5, of which waited for: 10 -> 1; matrix products, arithmetic and copies ran while one was open for 10% -> 7% of each run, Pallas kernels for 0% -> 76%
where the time goes in v4:
time: 178 us; the launch traced here: 176 us
  Pallas kernels  135 us (76%)
  waiting for transfers between devices  9.91 us (6%)
  matrix products  9.61 us (5%)
  starting transfers between devices  9.47 us (5%)
  other arithmetic  7.76 us (4%)
  local copies, waits for them, and re-layouts  4.02 us (2%)
    pallas_call x1, Pallas kernels, project(): pl.pallas_call(functools.partial(project_kernel, count), out_shape=jax.Sh...  135 us
    ppermute x3, waiting for transfers between devices, shards(): lax.ppermute(sent_state, 'seq', [(s, s + k) for s in range(seq_count - k)])  9.9 us
    ppermute x3, starting transfers between devices, shards(): lax.ppermute(sent_state, 'seq', [(s, s + k) for s in range(seq_count - k)])  7.6 us
    dot_general x1, matrix products, shards(): jnp.einsum('hts,shd->thd', weights, value_heads, preferred_element_type=f32)  5.2 us
  transfers between devices with their start and end apart: 5, of which 1 were waited for; matrix products, arithmetic and copies ran while one was open for 7% of the time, Pallas kernels for 76%

profile of v4, /device:TPU:11, one launch (start us, length us, event | category | flops | bytes accessed | tf_op | source)
XLA Modules:
  0.0 176.4 jit_solution(13915169726649178001)
XLA Ops:
  0.0 0.9 select_reduce_fusion.3
  0.9 0.7 multiply_exponential_fusion
  1.6 0.1 select_reduce_fusion.1
  1.7 0.6 slice.3
  3.0 1.5 copy.22
  4.5 0.1 exponential_select_fusion.1
  4.6 0.0 copy-done.4
  4.6 0.0 copy-start.3
  4.6 1.2 convolution_convert_fusion
  5.8 3.2 %collective-permute-start = (bf16[8,128,128]{2,1,0:T(8,128)(2,1)}, bf16[8,128,128]{2,1,0:T(8,128)(2,1)S(1)}, u32[]{:S(2)}, u32[]{:S(2)}) collective-permute-start(bf16[8,128,128]{2,1,0:T(8,128)(2,1)} %convolution_convert_fusion), channel_id=1, source_target_pairs={{0,4},{4,8},{8,12},{1,5},{5,9},{9,13},{2,6},{6,10},{10,14},{3,7},{... | collective-permute-start | bytes 786440 | tf_op jit(solution)/shard_map/ppermute | solution.py:245
  9.0 3.0 %collective-permute-start.1 = (bf16[8,128,128]{2,1,0:T(8,128)(2,1)}, bf16[8,128,128]{2,1,0:T(8,128)(2,1)}, u32[]{:S(2)}, u32[]{:S(2)}) collective-permute-start(bf16[8,128,128]{2,1,0:T(8,128)(2,1)} %convolution_convert_fusion), channel_id=1, source_target_pairs={{0,8},{4,12},{1,9},{5,13},{2,10},{6,14},{3,11},{7,15},{16,24},{20,... | collective-permute-start | bytes 786440 | tf_op jit(solution)/shard_map/ppermute | solution.py:245
  12.0 1.4 collective-permute-start.2
  13.4 1.0 fusion.17
  14.4 1.1 fusion.14
  15.5 0.2 select_reduce_fusion.2
  15.7 0.1 broadcast_select_fusion.1
  15.8 0.1 select_reduce_fusion
  15.9 5.2 %fusion = f32[8,512,128]{1,2,0:T(8,128)S(1)} fusion(f32[512,512]{1,0:T(8,128)} %fusion.14, f32[8]{0:T(128)S(1)} %get-tuple-element.6, pred[512,512]{1,0:T(8,128)(4,1)} %fusion.17, bf16[512,8,128]{0,2,1:T(8,128)(2,1)} %bitcast.46, bf16[512,1024]{1,0:T(8,128)(2,1)} %param.10, bf16[512,1024]{1,0:T(8,128)(2,1)S(1)} %copy-done), kind=kOutput, calls=%fused_computation.1 | convolution fusion | flops 1082130432 | bytes 6553632 | tf_op jit(solution)/shard_map/hts,shd->thd/dot_general | solution.py:267
  21.1 0.1 broadcast_select_fusion
  21.2 0.0 collective-permute-done
  21.2 9.9 %collective-permute-done.1 = bf16[8,128,128]{2,1,0:T(8,128)(2,1)} collective-permute-done((bf16[8,128,128]{2,1,0:T(8,128)(2,1)}, bf16[8,128,128]{2,1,0:T(8,128)(2,1)}, u32[]{:S(2)}, u32[]{:S(2)}) %collective-permute-start.1) | collective-permute-done | bytes 262176 | tf_op jit(solution)/shard_map/ppermute | solution.py:245
  31.1 0.0 collective-permute-done.2
  31.1 3.2 %multiply_reduce_fusion = (f32[512]{0:T(512)S(1)}, f32[512,8,128]{0,2,1:T(8,128)}) fusion(f32[512,8]{0,1:T(8,128)S(1)} %get-tuple-element.13, bf16[8,128,128]{2,1,0:T(8,128)(2,1)} %collective-permute-done.2, bf16[8,128,128]{2,1,0:T(8,128)(2,1)} %collective-permute-done.1, bf16[8,128,128]{2,1,0:T(8,128)(2,1)S(1)} %collective-permute-done, ...), kind=kOutput, calls=%fused_computation.10 | convolution fusion | flops 137494016 | bytes 6047840 | tf_op jit(solution)/shard_map/thd,hde->the/dot_general | solution.py:281
  34.3 1.6 collective-permute-start.3
  35.9 1.9 %copy.23 = f32[512,1024]{1,0:T(8,128)S(1)} copy(f32[512,1024]{0,1:T(8,128)} %bitcast.44) | data formatting | bytes 4194304 | tf_op jit(solution)/shard_map/reshape | solution.py:289
  37.8 0.0 copy-start.1
  37.8 2.0 %multiply_convert_fusion.3.g_ref = bf16[512,1024]{1,0:T(8,128)(2,1)S(1)} fusion(bf16[512,1024]{1,0:T(8,128)(2,1)} %param.11, f32[512,1024]{1,0:T(8,128)S(1)} %copy.23, f32[1024]{0:T(1024)S(1)} %convert_element_type.78), kind=kLoop, calls=%fused_computation.11 | loop fusion | flops 3670016 | bytes 4198400 | tf_op jit(solution)/shard_map/convert_element_type | solution.py:312
  39.8 0.0 collective-permute-done.3
  39.8 0.3 collective-permute-start.4
  40.1 134.7 %shard_map.82 = bf16[512,1536]{1,0:T(8,128)(2,1)S(1)} custom-call(bf16[512,1024]{1,0:T(8,128)(2,1)S(1)} %multiply_convert_fusion.3.g_ref, bf16[1536,1024]{1,0:T(8,128)(2,1)S(1)} %copy-done.1), custom_call_target="tpu_custom_call" | custom-call | flops 6442450944 | bytes 5767168 | tf_op jit(solution)/shard_map/pallas_call | solution.py:172
  174.9 0.0 collective-permute-done.4
  174.9 1.5 multiply_convert_fusion.2
  (19 shorter events, 0.1 us)
Async XLA Ops:
  0.0 15.9 %copy-start = (bf16[512,1024]{1,0:T(8,128)(2,1)S(1)}, bf16[512,1024]{1,0:T(8,128)(2,1)}, u32[]{:S(2)}) copy-start(bf16[512,1024]{1,0:T(8,128)(2,1)} %param.8) | copy-start | bytes 3145732
  0.0 4.6 %copy-start.4 = (bf16[512,1024]{1,0:T(8,128)(2,1)S(1)}, bf16[512,1024]{1,0:T(8,128)(2,1)}, u32[]{:S(2)}) copy-start(bf16[512,1024]{1,0:T(8,128)(2,1)} %param.10) | copy-start | bytes 3145732
  4.5 11.0 %copy-start.2 = (bf16[512,1024]{0,1:T(8,128)(2,1)}, bf16[512,1024]{0,1:T(8,128)(2,1)S(1)}, u32[]{:S(2)}) copy-start(bf16[512,1024]{0,1:T(8,128)(2,1)S(1)} %copy.22) | copy-start | bytes 3145732
  4.6 11.1 %copy-start.3 = (bf16[1024]{0:T(1024)(128)(2,1)S(1)}, bf16[1024]{0:T(1024)(128)(2,1)}, u32[]{:S(2)}) copy-start(bf16[1024]{0:T(1024)(128)(2,1)} %param.12) | copy-start | bytes 6148
  5.8 15.4 %collective-permute-start = (bf16[8,128,128]{2,1,0:T(8,128)(2,1)}, bf16[8,128,128]{2,1,0:T(8,128)(2,1)S(1)}, u32[]{:S(2)}, u32[]{:S(2)}) collective-permute-start(bf16[8,128,128]{2,1,0:T(8,128)(2,1)} %convolution_convert_fusion), channel_id=1, source_target_pairs={{0,4},{4,8},{8,12},{1,5},{5,9},{9,13},{2,6},{6,10},{10,14},{3,7},{... | collective-permute-start | bytes 786440 | tf_op jit(solution)/shard_map/ppermute | solution.py:245
  9.0 22.1 %collective-permute-start.1 = (bf16[8,128,128]{2,1,0:T(8,128)(2,1)}, bf16[8,128,128]{2,1,0:T(8,128)(2,1)}, u32[]{:S(2)}, u32[]{:S(2)}) collective-permute-start(bf16[8,128,128]{2,1,0:T(8,128)(2,1)} %convolution_convert_fusion), channel_id=1, source_target_pairs={{0,8},{4,12},{1,9},{5,13},{2,10},{6,14},{3,11},{7,15},{16,24},{20,... | collective-permute-start | bytes 786440 | tf_op jit(solution)/shard_map/ppermute | solution.py:245
  12.0 19.1 %collective-permute-start.2 = (bf16[8,128,128]{2,1,0:T(8,128)(2,1)}, bf16[8,128,128]{2,1,0:T(8,128)(2,1)}, u32[]{:S(2)}, u32[]{:S(2)}) collective-permute-start(bf16[8,128,128]{2,1,0:T(8,128)(2,1)} %convolution_convert_fusion), channel_id=1, source_target_pairs={{0,12},{1,13},{2,14},{3,15},{16,28},{17,29},{18,30},{19,31}} | collective-permute-start | bytes 786440 | tf_op jit(solution)/shard_map/ppermute | solution.py:245
  34.3 5.5 %collective-permute-start.3 = (f32[512]{0:T(512)S(1)}, f32[512]{0:T(512)S(1)}, u32[]{:S(2)}, u32[]{:S(2)}) collective-permute-start(f32[512]{0:T(512)S(1)} %get-tuple-element.14), channel_id=1, source_target_pairs={{0,1},{1,0},{2,3},{3,2},{4,5},{5,4},{6,7},{7,6},{8,9},{9,8},{10,11... | collective-permute-start | bytes 6152 | tf_op jit(solution)/shard_map/ppermute | solution.py:294
  37.8 2.3 %copy-start.1 = (bf16[1536,1024]{1,0:T(8,128)(2,1)S(1)}, bf16[1536,1024]{1,0:T(8,128)(2,1)}, u32[]{:S(2)}) copy-start(bf16[1536,1024]{1,0:T(8,128)(2,1)} %w_ref.1) | copy-start | bytes 9437188
  39.8 135.1 %collective-permute-start.4 = (f32[512]{0:T(512)S(1)}, f32[512]{0:T(512)S(1)}, u32[]{:S(2)}, u32[]{:S(2)}) collective-permute-start(f32[512]{0:T(512)S(1)} %add.77), channel_id=1, source_target_pairs={{0,2},{1,3},{2,0},{3,1},{4,6},{5,7},{6,4},{7,5},{8,10},{9,11},{10,... | collective-permute-start | bytes 6152 | tf_op jit(solution)/shard_map/ppermute | solution.py:294

commit v5 on v4

--- a/solution.py
+++ b/solution.py
@@ -114,17 +114,21 @@
         def _():
             out_ref[pl.ds(c * rows, rows), :] = send2[c]
 
-    start_hop(1, 0)
-    start_hop(1, 1)
+    def pump(k, c):
+        for way in (0, 1):
+            pl.when(comes(way, k))(lambda way=way: arrival(way, k, c).wait_recv())
+        if k < count - 1:
+            start_hop(k + 1, c)
+
+    for c in range(CHUNKS):
+        start_hop(1, c)
     given[me] = g_ref[...]
+    for k in range(1, count - 1):
+        pump(k, 0)
     for c in range(CHUNKS):
-        for k in range(1, count):
-            for way in (0, 1):
-                pl.when(comes(way, k))(lambda way=way: arrival(way, k, c).wait_recv())
-            if k < count - 1:
-                start_hop(k + 1, c)
-        if c + 2 < CHUNKS:
-            start_hop(1, c + 2)
+        pump(count - 1, c)
+        if c + 1 < CHUNKS:
+            pump(1, c + 1)
 
         for slot in range(2):
             def put_other(span, value):
@@ -134,6 +138,9 @@
             product(2 * side + 1 - core, c, put_other)
             pair_copy(0, slot, c).start()
 
+        if c + 1 < CHUNKS:
+            for k in range(2, count - 1):
+                pump(k, c + 1)
         pair_copy(0, 0, c).wait_recv()
 
         def put_far(span, value):

time: 178 us -> 178 us (level)
  no operation moved by 1% of the time
where the time goes in v5:
time: 178 us; the launch traced here: 176 us
  Pallas kernels  134 us (75%)
  waiting for transfers between devices  9.91 us (6%)
  matrix products  9.61 us (5%)
  starting transfers between devices  9.47 us (5%)
  other arithmetic  7.76 us (4%)
  local copies, waits for them, and re-layouts  4.02 us (2%)
    pallas_call x1, Pallas kernels, project(): pl.pallas_call(functools.partial(project_kernel, count), out_shape=jax.Sh...  134 us
    ppermute x3, waiting for transfers between devices, shards(): lax.ppermute(sent_state, 'seq', [(s, s + k) for s in range(seq_count - k)])  9.9 us
    ppermute x3, starting transfers between devices, shards(): lax.ppermute(sent_state, 'seq', [(s, s + k) for s in range(seq_count - k)])  7.6 us
    dot_general x1, matrix products, shards(): jnp.einsum('hts,shd->thd', weights, value_heads, preferred_element_type=f32)  5.2 us
  transfers between devices with their start and end apart: 5, of which 1 were waited for; matrix products, arithmetic and copies ran while one was open for 7% of the time, Pallas kernels for 76%

profile of v5, /device:TPU:11, one launch (start us, length us, event | category | flops | bytes accessed | tf_op | source)
XLA Modules:
  0.0 175.9 jit_solution(2288050589724020673)
XLA Ops:
  0.0 0.9 select_reduce_fusion.3
  0.9 0.7 multiply_exponential_fusion
  1.6 0.1 select_reduce_fusion.1
  1.7 0.6 slice.3
  3.0 1.5 copy.22
  4.5 0.1 exponential_select_fusion.1
  4.6 0.0 copy-start.3
  4.6 1.2 convolution_convert_fusion
  5.8 3.2 %collective-permute-start = (bf16[8,128,128]{2,1,0:T(8,128)(2,1)}, bf16[8,128,128]{2,1,0:T(8,128)(2,1)S(1)}, u32[]{:S(2)}, u32[]{:S(2)}) collective-permute-start(bf16[8,128,128]{2,1,0:T(8,128)(2,1)} %convolution_convert_fusion), channel_id=1, source_target_pairs={{0,4},{4,8},{8,12},{1,5},{5,9},{9,13},{2,6},{6,10},{10,14},{3,7},{... | collective-permute-start | bytes 786440 | tf_op jit(solution)/shard_map/ppermute | solution.py:252
  9.0 3.0 %collective-permute-start.1 = (bf16[8,128,128]{2,1,0:T(8,128)(2,1)}, bf16[8,128,128]{2,1,0:T(8,128)(2,1)}, u32[]{:S(2)}, u32[]{:S(2)}) collective-permute-start(bf16[8,128,128]{2,1,0:T(8,128)(2,1)} %convolution_convert_fusion), channel_id=1, source_target_pairs={{0,8},{4,12},{1,9},{5,13},{2,10},{6,14},{3,11},{7,15},{16,24},{20,... | collective-permute-start | bytes 786440 | tf_op jit(solution)/shard_map/ppermute | solution.py:252
  12.0 1.4 collective-permute-start.2
  13.4 1.0 fusion.17
  14.4 1.1 fusion.14
  15.5 0.2 select_reduce_fusion.2
  15.7 0.1 broadcast_select_fusion.1
  15.8 0.1 select_reduce_fusion
  15.9 0.0 copy-done
  15.9 5.2 %fusion = f32[8,512,128]{1,2,0:T(8,128)S(1)} fusion(f32[512,512]{1,0:T(8,128)} %fusion.14, f32[8]{0:T(128)S(1)} %get-tuple-element.6, pred[512,512]{1,0:T(8,128)(4,1)} %fusion.17, bf16[512,8,128]{0,2,1:T(8,128)(2,1)} %bitcast.46, bf16[512,1024]{1,0:T(8,128)(2,1)} %param.10, bf16[512,1024]{1,0:T(8,128)(2,1)S(1)} %copy-done), kind=kOutput, calls=%fused_computation.1 | convolution fusion | flops 1082130432 | bytes 6553632 | tf_op jit(solution)/shard_map/hts,shd->thd/dot_general | solution.py:274
  21.1 0.1 broadcast_select_fusion
  21.2 0.0 collective-permute-done
  21.2 9.9 %collective-permute-done.1 = bf16[8,128,128]{2,1,0:T(8,128)(2,1)} collective-permute-done((bf16[8,128,128]{2,1,0:T(8,128)(2,1)}, bf16[8,128,128]{2,1,0:T(8,128)(2,1)}, u32[]{:S(2)}, u32[]{:S(2)}) %collective-permute-start.1) | collective-permute-done | bytes 262176 | tf_op jit(solution)/shard_map/ppermute | solution.py:252
  31.1 0.0 collective-permute-done.2
  31.1 3.2 %multiply_reduce_fusion = (f32[512]{0:T(512)S(1)}, f32[512,8,128]{0,2,1:T(8,128)}) fusion(f32[512,8]{0,1:T(8,128)S(1)} %get-tuple-element.13, bf16[8,128,128]{2,1,0:T(8,128)(2,1)} %collective-permute-done.2, bf16[8,128,128]{2,1,0:T(8,128)(2,1)} %collective-permute-done.1, bf16[8,128,128]{2,1,0:T(8,128)(2,1)S(1)} %collective-permute-done, ...), kind=kOutput, calls=%fused_computation.10 | convolution fusion | flops 137494016 | bytes 6047840 | tf_op jit(solution)/shard_map/thd,hde->the/dot_general | solution.py:288
  34.3 1.6 collective-permute-start.3
  35.9 1.9 %copy.23 = f32[512,1024]{1,0:T(8,128)S(1)} copy(f32[512,1024]{0,1:T(8,128)} %bitcast.44) | data formatting | bytes 4194304 | tf_op jit(solution)/shard_map/reshape | solution.py:296
  37.8 0.0 copy-start.1
  37.8 2.0 %multiply_convert_fusion.3.g_ref = bf16[512,1024]{1,0:T(8,128)(2,1)S(1)} fusion(bf16[512,1024]{1,0:T(8,128)(2,1)} %param.11, f32[512,1024]{1,0:T(8,128)S(1)} %copy.23, f32[1024]{0:T(1024)S(1)} %convert_element_type.78), kind=kLoop, calls=%fused_computation.11 | loop fusion | flops 3670016 | bytes 4198400 | tf_op jit(solution)/shard_map/convert_element_type | solution.py:319
  39.8 0.0 collective-permute-done.3
  39.8 0.3 collective-permute-start.4
  40.1 134.3 %shard_map.82 = bf16[512,1536]{1,0:T(8,128)(2,1)S(1)} custom-call(bf16[512,1024]{1,0:T(8,128)(2,1)S(1)} %multiply_convert_fusion.3.g_ref, bf16[1536,1024]{1,0:T(8,128)(2,1)S(1)} %copy-done.1), custom_call_target="tpu_custom_call" | custom-call | flops 6442450944 | bytes 5767168 | tf_op jit(solution)/shard_map/pallas_call | solution.py:179
  174.4 0.0 collective-permute-done.4
  174.4 1.5 multiply_convert_fusion.2
  (19 shorter events, 0.1 us)
Async XLA Ops:
  0.0 15.9 %copy-start = (bf16[512,1024]{1,0:T(8,128)(2,1)S(1)}, bf16[512,1024]{1,0:T(8,128)(2,1)}, u32[]{:S(2)}) copy-start(bf16[512,1024]{1,0:T(8,128)(2,1)} %param.8) | copy-start | bytes 3145732
  0.0 4.6 %copy-start.4 = (bf16[512,1024]{1,0:T(8,128)(2,1)S(1)}, bf16[512,1024]{1,0:T(8,128)(2,1)}, u32[]{:S(2)}) copy-start(bf16[512,1024]{1,0:T(8,128)(2,1)} %param.10) | copy-start | bytes 3145732
  4.5 11.0 %copy-start.2 = (bf16[512,1024]{0,1:T(8,128)(2,1)}, bf16[512,1024]{0,1:T(8,128)(2,1)S(1)}, u32[]{:S(2)}) copy-start(bf16[512,1024]{0,1:T(8,128)(2,1)S(1)} %copy.22) | copy-start | bytes 3145732
  4.6 11.1 %copy-start.3 = (bf16[1024]{0:T(1024)(128)(2,1)S(1)}, bf16[1024]{0:T(1024)(128)(2,1)}, u32[]{:S(2)}) copy-start(bf16[1024]{0:T(1024)(128)(2,1)} %param.12) | copy-start | bytes 6148
  5.8 15.4 %collective-permute-start = (bf16[8,128,128]{2,1,0:T(8,128)(2,1)}, bf16[8,128,128]{2,1,0:T(8,128)(2,1)S(1)}, u32[]{:S(2)}, u32[]{:S(2)}) collective-permute-start(bf16[8,128,128]{2,1,0:T(8,128)(2,1)} %convolution_convert_fusion), channel_id=1, source_target_pairs={{0,4},{4,8},{8,12},{1,5},{5,9},{9,13},{2,6},{6,10},{10,14},{3,7},{... | collective-permute-start | bytes 786440 | tf_op jit(solution)/shard_map/ppermute | solution.py:252
  9.0 22.1 %collective-permute-start.1 = (bf16[8,128,128]{2,1,0:T(8,128)(2,1)}, bf16[8,128,128]{2,1,0:T(8,128)(2,1)}, u32[]{:S(2)}, u32[]{:S(2)}) collective-permute-start(bf16[8,128,128]{2,1,0:T(8,128)(2,1)} %convolution_convert_fusion), channel_id=1, source_target_pairs={{0,8},{4,12},{1,9},{5,13},{2,10},{6,14},{3,11},{7,15},{16,24},{20,... | collective-permute-start | bytes 786440 | tf_op jit(solution)/shard_map/ppermute | solution.py:252
  12.0 19.1 %collective-permute-start.2 = (bf16[8,128,128]{2,1,0:T(8,128)(2,1)}, bf16[8,128,128]{2,1,0:T(8,128)(2,1)}, u32[]{:S(2)}, u32[]{:S(2)}) collective-permute-start(bf16[8,128,128]{2,1,0:T(8,128)(2,1)} %convolution_convert_fusion), channel_id=1, source_target_pairs={{0,12},{1,13},{2,14},{3,15},{16,28},{17,29},{18,30},{19,31}} | collective-permute-start | bytes 786440 | tf_op jit(solution)/shard_map/ppermute | solution.py:252
  34.3 5.5 %collective-permute-start.3 = (f32[512]{0:T(512)S(1)}, f32[512]{0:T(512)S(1)}, u32[]{:S(2)}, u32[]{:S(2)}) collective-permute-start(f32[512]{0:T(512)S(1)} %get-tuple-element.14), channel_id=1, source_target_pairs={{0,1},{1,0},{2,3},{3,2},{4,5},{5,4},{6,7},{7,6},{8,9},{9,8},{10,11... | collective-permute-start | bytes 6152 | tf_op jit(solution)/shard_map/ppermute | solution.py:301
  37.8 2.3 %copy-start.1 = (bf16[1536,1024]{1,0:T(8,128)(2,1)S(1)}, bf16[1536,1024]{1,0:T(8,128)(2,1)}, u32[]{:S(2)}) copy-start(bf16[1536,1024]{1,0:T(8,128)(2,1)} %w_ref.1) | copy-start | bytes 9437188
  39.8 134.6 %collective-permute-start.4 = (f32[512]{0:T(512)S(1)}, f32[512]{0:T(512)S(1)}, u32[]{:S(2)}, u32[]{:S(2)}) collective-permute-start(f32[512]{0:T(512)S(1)} %add.77), channel_id=1, source_target_pairs={{0,2},{1,3},{2,0},{3,1},{4,6},{5,7},{6,4},{7,5},{8,10},{9,11},{10,... | collective-permute-start | bytes 6152 | tf_op jit(solution)/shard_map/ppermute | solution.py:301

commit v6 on v5

--- a/solution.py
+++ b/solution.py
@@ -8,7 +8,7 @@
 from jax.sharding import PartitionSpec as P
 
 HEAD_DIM = 128
-CHUNKS = 4
+CHUNKS = 8
 
 MESH = pl.DeviceIdType.MESH
 

time: 178 us -> 178 us (level)
  the two profiles are of different devices: /device:TPU:11 before, /device:TPU:20 now
where the time goes in v6:
time: 178 us
  Pallas kernels  139 us (78%)
  matrix products  9.62 us (5%)
  waiting for transfers between devices  8.55 us (5%)
  other arithmetic  7.76 us (4%)
  starting transfers between devices  7.73 us (4%)
  local copies, waits for them, and re-layouts  4.02 us (2%)
    pallas_call x1, Pallas kernels, project(): pl.pallas_call(functools.partial(project_kernel, count), out_shape=jax.Sh...  139 us
    ppermute x3, waiting for transfers between devices, shards(): lax.ppermute(sent_state, 'seq', [(s, s + k) for s in range(seq_count - k)])  8.55 us
    ppermute x3, starting transfers between devices, shards(): lax.ppermute(sent_state, 'seq', [(s, s + k) for s in range(seq_count - k)])  6.17 us
    dot_general x1, matrix products, shards(): jnp.einsum('hts,shd->thd', weights, value_heads, preferred_element_type=f32)  5.2 us
  transfers between devices with their start and end apart: 5, of which 1 were waited for; matrix products, arithmetic and copies ran while one was open for 7% of the time, Pallas kernels for 78%

profile of v6, /device:TPU:20, one launch (start us, length us, event | category | flops | bytes accessed | tf_op | source)
XLA Modules:
  0.0 177.8 jit_solution(9711652229605241578)
XLA Ops:
  0.0 0.0 copy-start
  0.0 0.9 select_reduce_fusion.3
  0.9 0.7 multiply_exponential_fusion
  1.6 0.1 select_reduce_fusion.1
  1.7 0.6 slice.3
  3.0 1.5 copy.22
  4.5 0.1 exponential_select_fusion.1
  4.6 0.0 copy-start.3
  4.6 1.2 convolution_convert_fusion
  5.8 3.5 %collective-permute-start = (bf16[8,128,128]{2,1,0:T(8,128)(2,1)}, bf16[8,128,128]{2,1,0:T(8,128)(2,1)S(1)}, u32[]{:S(2)}, u32[]{:S(2)}) collective-permute-start(bf16[8,128,128]{2,1,0:T(8,128)(2,1)} %convolution_convert_fusion), channel_id=1, source_target_pairs={{0,4},{4,8},{8,12},{1,5},{5,9},{9,13},{2,6},{6,10},{10,14},{3,7},{... | collective-permute-start | bytes 786440 | tf_op jit(solution)/shard_map/ppermute | solution.py:252
  9.3 1.3 collective-permute-start.1
  10.6 1.4 collective-permute-start.2
  12.0 1.0 fusion.17
  13.0 1.1 fusion.14
  14.1 0.2 select_reduce_fusion.2
  14.3 0.1 broadcast_select_fusion.1
  14.4 0.1 select_reduce_fusion
  14.5 5.2 %fusion = f32[8,512,128]{1,2,0:T(8,128)S(1)} fusion(f32[512,512]{1,0:T(8,128)} %fusion.14, f32[8]{0:T(128)S(1)} %get-tuple-element.6, pred[512,512]{1,0:T(8,128)(4,1)} %fusion.17, bf16[512,8,128]{0,2,1:T(8,128)(2,1)} %bitcast.46, bf16[512,1024]{1,0:T(8,128)(2,1)} %param.10, bf16[512,1024]{1,0:T(8,128)(2,1)S(1)} %copy-done), kind=kOutput, calls=%fused_computation.1 | convolution fusion | flops 1082130432 | bytes 6553632 | tf_op jit(solution)/shard_map/hts,shd->thd/dot_general | solution.py:274
  19.7 0.1 broadcast_select_fusion
  19.8 8.5 %collective-permute-done = bf16[8,128,128]{2,1,0:T(8,128)(2,1)S(1)} collective-permute-done((bf16[8,128,128]{2,1,0:T(8,128)(2,1)}, bf16[8,128,128]{2,1,0:T(8,128)(2,1)S(1)}, u32[]{:S(2)}, u32[]{:S(2)}) %collective-permute-start) | collective-permute-done | bytes 262176 | tf_op jit(solution)/shard_map/ppermute | solution.py:252
  28.3 0.0 collective-permute-done.1
  28.3 0.0 collective-permute-done.2
  28.3 3.2 %multiply_reduce_fusion = (f32[512]{0:T(512)S(1)}, f32[512,8,128]{0,2,1:T(8,128)}) fusion(f32[512,8]{0,1:T(8,128)S(1)} %get-tuple-element.13, bf16[8,128,128]{2,1,0:T(8,128)(2,1)} %collective-permute-done.2, bf16[8,128,128]{2,1,0:T(8,128)(2,1)} %collective-permute-done.1, bf16[8,128,128]{2,1,0:T(8,128)(2,1)S(1)} %collective-permute-done, ...), kind=kOutput, calls=%fused_computation.10 | convolution fusion | flops 137494016 | bytes 6047840 | tf_op jit(solution)/shard_map/thd,hde->the/dot_general | solution.py:288
  31.5 0.0 collective-permute-start.3
  31.5 1.9 %copy.23 = f32[512,1024]{1,0:T(8,128)S(1)} copy(f32[512,1024]{0,1:T(8,128)} %bitcast.44) | data formatting | bytes 4194304 | tf_op jit(solution)/shard_map/reshape | solution.py:296
  33.5 0.0 copy-start.1
  33.5 2.0 %multiply_convert_fusion.3.g_ref = bf16[512,1024]{1,0:T(8,128)(2,1)S(1)} fusion(bf16[512,1024]{1,0:T(8,128)(2,1)} %param.11, f32[512,1024]{1,0:T(8,128)S(1)} %copy.23, f32[1024]{0:T(1024)S(1)} %convert_element_type.78), kind=kLoop, calls=%fused_computation.11 | loop fusion | flops 3670016 | bytes 4198400 | tf_op jit(solution)/shard_map/convert_element_type | solution.py:319
  35.4 0.0 collective-permute-done.3
  35.5 1.6 collective-permute-start.4
  37.0 139.3 %shard_map.82 = bf16[512,1536]{1,0:T(8,128)(2,1)S(1)} custom-call(bf16[512,1024]{1,0:T(8,128)(2,1)S(1)} %multiply_convert_fusion.3.g_ref, bf16[1536,1024]{1,0:T(8,128)(2,1)S(1)} %copy-done.1), custom_call_target="tpu_custom_call" | custom-call | flops 6442450944 | bytes 5767168 | tf_op jit(solution)/shard_map/pallas_call | solution.py:179
  176.4 0.0 collective-permute-done.4
  176.4 1.5 multiply_convert_fusion.2
  (19 shorter events, 0.1 us)
Async XLA Ops:
  0.0 14.5 %copy-start = (bf16[512,1024]{1,0:T(8,128)(2,1)S(1)}, bf16[512,1024]{1,0:T(8,128)(2,1)}, u32[]{:S(2)}) copy-start(bf16[512,1024]{1,0:T(8,128)(2,1)} %param.8) | copy-start | bytes 3145732
  0.0 4.6 %copy-start.4 = (bf16[512,1024]{1,0:T(8,128)(2,1)S(1)}, bf16[512,1024]{1,0:T(8,128)(2,1)}, u32[]{:S(2)}) copy-start(bf16[512,1024]{1,0:T(8,128)(2,1)} %param.10) | copy-start | bytes 3145732
  4.5 9.6 %copy-start.2 = (bf16[512,1024]{0,1:T(8,128)(2,1)}, bf16[512,1024]{0,1:T(8,128)(2,1)S(1)}, u32[]{:S(2)}) copy-start(bf16[512,1024]{0,1:T(8,128)(2,1)S(1)} %copy.22) | copy-start | bytes 3145732
  4.6 9.7 %copy-start.3 = (bf16[1024]{0:T(1024)(128)(2,1)S(1)}, bf16[1024]{0:T(1024)(128)(2,1)}, u32[]{:S(2)}) copy-start(bf16[1024]{0:T(1024)(128)(2,1)} %param.12) | copy-start | bytes 6148
  5.8 22.5 %collective-permute-start = (bf16[8,128,128]{2,1,0:T(8,128)(2,1)}, bf16[8,128,128]{2,1,0:T(8,128)(2,1)S(1)}, u32[]{:S(2)}, u32[]{:S(2)}) collective-permute-start(bf16[8,128,128]{2,1,0:T(8,128)(2,1)} %convolution_convert_fusion), channel_id=1, source_target_pairs={{0,4},{4,8},{8,12},{1,5},{5,9},{9,13},{2,6},{6,10},{10,14},{3,7},{... | collective-permute-start | bytes 786440 | tf_op jit(solution)/shard_map/ppermute | solution.py:252
  9.3 19.0 %collective-permute-start.1 = (bf16[8,128,128]{2,1,0:T(8,128)(2,1)}, bf16[8,128,128]{2,1,0:T(8,128)(2,1)}, u32[]{:S(2)}, u32[]{:S(2)}) collective-permute-start(bf16[8,128,128]{2,1,0:T(8,128)(2,1)} %convolution_convert_fusion), channel_id=1, source_target_pairs={{0,8},{4,12},{1,9},{5,13},{2,10},{6,14},{3,11},{7,15},{16,24},{20,... | collective-permute-start | bytes 786440 | tf_op jit(solution)/shard_map/ppermute | solution.py:252
  10.6 17.7 %collective-permute-start.2 = (bf16[8,128,128]{2,1,0:T(8,128)(2,1)}, bf16[8,128,128]{2,1,0:T(8,128)(2,1)}, u32[]{:S(2)}, u32[]{:S(2)}) collective-permute-start(bf16[8,128,128]{2,1,0:T(8,128)(2,1)} %convolution_convert_fusion), channel_id=1, source_target_pairs={{0,12},{1,13},{2,14},{3,15},{16,28},{17,29},{18,30},{19,31}} | collective-permute-start | bytes 786440 | tf_op jit(solution)/shard_map/ppermute | solution.py:252
  31.5 3.9 %collective-permute-start.3 = (f32[512]{0:T(512)S(1)}, f32[512]{0:T(512)S(1)}, u32[]{:S(2)}, u32[]{:S(2)}) collective-permute-start(f32[512]{0:T(512)S(1)} %get-tuple-element.14), channel_id=1, source_target_pairs={{0,1},{1,0},{2,3},{3,2},{4,5},{5,4},{6,7},{7,6},{8,9},{9,8},{10,11... | collective-permute-start | bytes 6152 | tf_op jit(solution)/shard_map/ppermute | solution.py:301
  33.5 3.6 %copy-start.1 = (bf16[1536,1024]{1,0:T(8,128)(2,1)S(1)}, bf16[1536,1024]{1,0:T(8,128)(2,1)}, u32[]{:S(2)}) copy-start(bf16[1536,1024]{1,0:T(8,128)(2,1)} %w_ref.1) | copy-start | bytes 9437188
  35.5 140.9 %collective-permute-start.4 = (f32[512]{0:T(512)S(1)}, f32[512]{0:T(512)S(1)}, u32[]{:S(2)}, u32[]{:S(2)}) collective-permute-start(f32[512]{0:T(512)S(1)} %add.77), channel_id=1, source_target_pairs={{0,2},{1,3},{2,0},{3,1},{4,6},{5,7},{6,4},{7,5},{8,10},{9,11},{10,... | collective-permute-start | bytes 6152 | tf_op jit(solution)/shard_map/ppermute | solution.py:301

commit v7 on v6

--- a/solution.py
+++ b/solution.py
@@ -8,7 +8,7 @@
 from jax.sharding import PartitionSpec as P
 
 HEAD_DIM = 128
-CHUNKS = 8
+CHUNKS = 2
 
 MESH = pl.DeviceIdType.MESH
 

time: 178 us -> 190 us (1.067)
  the two profiles are of different devices: /device:TPU:20 before, /device:TPU:11 now
where the time goes in v7:
time: 190 us; the launch traced here: 189 us
  Pallas kernels  148 us (78%)
  waiting for transfers between devices  9.91 us (5%)
  matrix products  9.61 us (5%)
  starting transfers between devices  9.47 us (5%)
  other arithmetic  7.76 us (4%)
  local copies, waits for them, and re-layouts  4.02 us (2%)
    pallas_call x1, Pallas kernels, project(): pl.pallas_call(functools.partial(project_kernel, count), out_shape=jax.Sh...  148 us
    ppermute x3, waiting for transfers between devices, shards(): lax.ppermute(sent_state, 'seq', [(s, s + k) for s in range(seq_count - k)])  9.9 us
    ppermute x3, starting transfers between devices, shards(): lax.ppermute(sent_state, 'seq', [(s, s + k) for s in range(seq_count - k)])  7.6 us
    dot_general x1, matrix products, shards(): jnp.einsum('hts,shd->thd', weights, value_heads, preferred_element_type=f32)  5.2 us
  transfers between devices with their start and end apart: 5, of which 1 were waited for; matrix products, arithmetic and copies ran while one was open for 6% of the time, Pallas kernels for 78%

profile of v7, /device:TPU:11, one launch (start us, length us, event | category | flops | bytes accessed | tf_op | source)
XLA Modules:
  0.0 189.4 jit_solution(142176176727769187)
XLA Ops:
  0.0 0.9 select_reduce_fusion.3
  0.9 0.7 multiply_exponential_fusion
  1.6 0.1 select_reduce_fusion.1
  1.7 0.6 slice.3
  3.0 1.5 copy.22
  4.5 0.1 exponential_select_fusion.1
  4.6 0.0 copy-done.4
  4.6 0.0 copy-start.3
  4.6 1.2 convolution_convert_fusion
  5.8 3.2 %collective-permute-start = (bf16[8,128,128]{2,1,0:T(8,128)(2,1)}, bf16[8,128,128]{2,1,0:T(8,128)(2,1)S(1)}, u32[]{:S(2)}, u32[]{:S(2)}) collective-permute-start(bf16[8,128,128]{2,1,0:T(8,128)(2,1)} %convolution_convert_fusion), channel_id=1, source_target_pairs={{0,4},{4,8},{8,12},{1,5},{5,9},{9,13},{2,6},{6,10},{10,14},{3,7},{... | collective-permute-start | bytes 786440 | tf_op jit(solution)/shard_map/ppermute | solution.py:252
  9.0 3.0 %collective-permute-start.1 = (bf16[8,128,128]{2,1,0:T(8,128)(2,1)}, bf16[8,128,128]{2,1,0:T(8,128)(2,1)}, u32[]{:S(2)}, u32[]{:S(2)}) collective-permute-start(bf16[8,128,128]{2,1,0:T(8,128)(2,1)} %convolution_convert_fusion), channel_id=1, source_target_pairs={{0,8},{4,12},{1,9},{5,13},{2,10},{6,14},{3,11},{7,15},{16,24},{20,... | collective-permute-start | bytes 786440 | tf_op jit(solution)/shard_map/ppermute | solution.py:252
  12.0 1.4 collective-permute-start.2
  13.4 1.0 fusion.17
  14.4 1.1 fusion.14
  15.5 0.2 select_reduce_fusion.2
  15.7 0.1 broadcast_select_fusion.1
  15.8 0.1 select_reduce_fusion
  15.9 5.2 %fusion = f32[8,512,128]{1,2,0:T(8,128)S(1)} fusion(f32[512,512]{1,0:T(8,128)} %fusion.14, f32[8]{0:T(128)S(1)} %get-tuple-element.6, pred[512,512]{1,0:T(8,128)(4,1)} %fusion.17, bf16[512,8,128]{0,2,1:T(8,128)(2,1)} %bitcast.46, bf16[512,1024]{1,0:T(8,128)(2,1)} %param.10, bf16[512,1024]{1,0:T(8,128)(2,1)S(1)} %copy-done), kind=kOutput, calls=%fused_computation.1 | convolution fusion | flops 1082130432 | bytes 6553632 | tf_op jit(solution)/shard_map/hts,shd->thd/dot_general | solution.py:274
  21.1 0.1 broadcast_select_fusion
  21.2 0.0 collective-permute-done
  21.2 9.9 %collective-permute-done.1 = bf16[8,128,128]{2,1,0:T(8,128)(2,1)} collective-permute-done((bf16[8,128,128]{2,1,0:T(8,128)(2,1)}, bf16[8,128,128]{2,1,0:T(8,128)(2,1)}, u32[]{:S(2)}, u32[]{:S(2)}) %collective-permute-start.1) | collective-permute-done | bytes 262176 | tf_op jit(solution)/shard_map/ppermute | solution.py:252
  31.1 0.0 collective-permute-done.2
  31.1 3.2 %multiply_reduce_fusion = (f32[512]{0:T(512)S(1)}, f32[512,8,128]{0,2,1:T(8,128)}) fusion(f32[512,8]{0,1:T(8,128)S(1)} %get-tuple-element.13, bf16[8,128,128]{2,1,0:T(8,128)(2,1)} %collective-permute-done.2, bf16[8,128,128]{2,1,0:T(8,128)(2,1)} %collective-permute-done.1, bf16[8,128,128]{2,1,0:T(8,128)(2,1)S(1)} %collective-permute-done, ...), kind=kOutput, calls=%fused_computation.10 | convolution fusion | flops 137494016 | bytes 6047840 | tf_op jit(solution)/shard_map/thd,hde->the/dot_general | solution.py:288
  34.3 1.6 collective-permute-start.3
  35.9 1.9 %copy.23 = f32[512,1024]{1,0:T(8,128)S(1)} copy(f32[512,1024]{0,1:T(8,128)} %bitcast.44) | data formatting | bytes 4194304 | tf_op jit(solution)/shard_map/reshape | solution.py:296
  37.8 0.0 copy-start.1
  37.8 2.0 %multiply_convert_fusion.3.g_ref = bf16[512,1024]{1,0:T(8,128)(2,1)S(1)} fusion(bf16[512,1024]{1,0:T(8,128)(2,1)} %param.11, f32[512,1024]{1,0:T(8,128)S(1)} %copy.23, f32[1024]{0:T(1024)S(1)} %convert_element_type.78), kind=kLoop, calls=%fused_computation.11 | loop fusion | flops 3670016 | bytes 4198400 | tf_op jit(solution)/shard_map/convert_element_type | solution.py:319
  39.8 0.0 collective-permute-done.3
  39.8 0.3 collective-permute-start.4
  40.1 147.8 %shard_map.82 = bf16[512,1536]{1,0:T(8,128)(2,1)S(1)} custom-call(bf16[512,1024]{1,0:T(8,128)(2,1)S(1)} %multiply_convert_fusion.3.g_ref, bf16[1536,1024]{1,0:T(8,128)(2,1)S(1)} %copy-done.1), custom_call_target="tpu_custom_call" | custom-call | flops 6442450944 | bytes 5767168 | tf_op jit(solution)/shard_map/pallas_call | solution.py:179
  187.9 0.0 collective-permute-done.4
  187.9 1.5 multiply_convert_fusion.2
  (19 shorter events, 0.1 us)
Async XLA Ops:
  0.0 15.9 %copy-start = (bf16[512,1024]{1,0:T(8,128)(2,1)S(1)}, bf16[512,1024]{1,0:T(8,128)(2,1)}, u32[]{:S(2)}) copy-start(bf16[512,1024]{1,0:T(8,128)(2,1)} %param.8) | copy-start | bytes 3145732
  0.0 4.6 %copy-start.4 = (bf16[512,1024]{1,0:T(8,128)(2,1)S(1)}, bf16[512,1024]{1,0:T(8,128)(2,1)}, u32[]{:S(2)}) copy-start(bf16[512,1024]{1,0:T(8,128)(2,1)} %param.10) | copy-start | bytes 3145732
  4.5 11.0 %copy-start.2 = (bf16[512,1024]{0,1:T(8,128)(2,1)}, bf16[512,1024]{0,1:T(8,128)(2,1)S(1)}, u32[]{:S(2)}) copy-start(bf16[512,1024]{0,1:T(8,128)(2,1)S(1)} %copy.22) | copy-start | bytes 3145732
  4.6 11.1 %copy-start.3 = (bf16[1024]{0:T(1024)(128)(2,1)S(1)}, bf16[1024]{0:T(1024)(128)(2,1)}, u32[]{:S(2)}) copy-start(bf16[1024]{0:T(1024)(128)(2,1)} %param.12) | copy-start | bytes 6148
  5.8 15.4 %collective-permute-start = (bf16[8,128,128]{2,1,0:T(8,128)(2,1)}, bf16[8,128,128]{2,1,0:T(8,128)(2,1)S(1)}, u32[]{:S(2)}, u32[]{:S(2)}) collective-permute-start(bf16[8,128,128]{2,1,0:T(8,128)(2,1)} %convolution_convert_fusion), channel_id=1, source_target_pairs={{0,4},{4,8},{8,12},{1,5},{5,9},{9,13},{2,6},{6,10},{10,14},{3,7},{... | collective-permute-start | bytes 786440 | tf_op jit(solution)/shard_map/ppermute | solution.py:252
  9.0 22.1 %collective-permute-start.1 = (bf16[8,128,128]{2,1,0:T(8,128)(2,1)}, bf16[8,128,128]{2,1,0:T(8,128)(2,1)}, u32[]{:S(2)}, u32[]{:S(2)}) collective-permute-start(bf16[8,128,128]{2,1,0:T(8,128)(2,1)} %convolution_convert_fusion), channel_id=1, source_target_pairs={{0,8},{4,12},{1,9},{5,13},{2,10},{6,14},{3,11},{7,15},{16,24},{20,... | collective-permute-start | bytes 786440 | tf_op jit(solution)/shard_map/ppermute | solution.py:252
  12.0 19.1 %collective-permute-start.2 = (bf16[8,128,128]{2,1,0:T(8,128)(2,1)}, bf16[8,128,128]{2,1,0:T(8,128)(2,1)}, u32[]{:S(2)}, u32[]{:S(2)}) collective-permute-start(bf16[8,128,128]{2,1,0:T(8,128)(2,1)} %convolution_convert_fusion), channel_id=1, source_target_pairs={{0,12},{1,13},{2,14},{3,15},{16,28},{17,29},{18,30},{19,31}} | collective-permute-start | bytes 786440 | tf_op jit(solution)/shard_map/ppermute | solution.py:252
  34.3 5.5 %collective-permute-start.3 = (f32[512]{0:T(512)S(1)}, f32[512]{0:T(512)S(1)}, u32[]{:S(2)}, u32[]{:S(2)}) collective-permute-start(f32[512]{0:T(512)S(1)} %get-tuple-element.14), channel_id=1, source_target_pairs={{0,1},{1,0},{2,3},{3,2},{4,5},{5,4},{6,7},{7,6},{8,9},{9,8},{10,11... | collective-permute-start | bytes 6152 | tf_op jit(solution)/shard_map/ppermute | solution.py:301
  37.8 2.3 %copy-start.1 = (bf16[1536,1024]{1,0:T(8,128)(2,1)S(1)}, bf16[1536,1024]{1,0:T(8,128)(2,1)}, u32[]{:S(2)}) copy-start(bf16[1536,1024]{1,0:T(8,128)(2,1)} %w_ref.1) | copy-start | bytes 9437188
  39.8 148.1 %collective-permute-start.4 = (f32[512]{0:T(512)S(1)}, f32[512]{0:T(512)S(1)}, u32[]{:S(2)}, u32[]{:S(2)}) collective-permute-start(f32[512]{0:T(512)S(1)} %add.77), channel_id=1, source_target_pairs={{0,2},{1,3},{2,0},{3,1},{4,6},{5,7},{6,4},{7,5},{8,10},{9,11},{10,... | collective-permute-start | bytes 6152 | tf_op jit(solution)/shard_map/ppermute | solution.py:301
